TPU v7x, 32 devices: a whole 2x2x4 slice. The times are simulated.
32 devices in a mesh: az: 16 (over z, y, core), rad: 2 (over x).
Axes of the slice: x: 2, y: 2, z: 4, core: 2. Of those that a mesh axis runs over, the one named last changes fastest.
Arguments:
- fluid_state: float32 [5, 2, 128, 2048], P(None, None, 'rad', 'az'), may hold values from -6 to 6
- velocity: float32 [2, 2, 128, 2048], P(None, None, 'rad', 'az'), may hold values from -0.4 to 0.4
- shifts: int32 [128], P('rad'), may hold values from 0 to 160, as said below
- fraction: float32 [128], P('rad'), may hold values from 0 to 1
Outputs:
- advected: float32 [5, 2, 128, 2048], P(None, None, 'rad', 'az')
Inputs may be any that keep to these rules, and one draw needn't show every extreme that they name: `shifts`: in every draw some cycle has shift 160 and some cycle has shift 0.
All inputs are finite; a program needn't handle non-finite values.
Results may differ from a plain program's by a relative error of at most 0.00002.
Values sent between devices are 32-bit elements; how exact they have to be, the bound alone decides.
A program may use at most 64 MiB of HBM per device.

v0:
```python
import jax
import jax.numpy as jnp
from jax import lax
from jax.sharding import PartitionSpec as P

STEPS = 2


def with_halo(x, sides, width, wrap):
    for axis, dim in sides:
        peers, length = (lax.axis_size(axis), x.shape[dim])
        up = [(i, (i + 1) % peers) for i in range(peers if wrap else peers - 1)]
        down = [(j, i) for i, j in up]
        last = lax.slice_in_dim(x, length - width, length, axis=dim)
        first = lax.slice_in_dim(x, 0, width, axis=dim)
        before = lax.ppermute(last, axis, up)
        after = lax.ppermute(first, axis, down)
        x = jnp.concatenate([before, x, after], axis=dim)
    return x


def shifted(value, axis, steps):
    count = lax.axis_size(axis)
    pairs = [(source, (source + steps) % count) for source in range(count)]
    return lax.ppermute(value, axis, pairs)


def tendency(padded, velocity_pad):
    radial_speed = velocity_pad[0]
    cycle_speed = velocity_pad[1]
    face_radial = 0.5 * (radial_speed[..., :-1, 1:-1] + radial_speed[..., 1:, 1:-1])
    flux_radial = (
        jnp.maximum(face_radial, 0.0) * padded[..., :-1, 1:-1]
        + jnp.minimum(face_radial, 0.0) * padded[..., 1:, 1:-1]
    )
    face_cycle = 0.5 * (cycle_speed[..., 1:-1, :-1] + cycle_speed[..., 1:-1, 1:])
    flux_cycle = (
        jnp.maximum(face_cycle, 0.0) * padded[..., 1:-1, :-1]
        + jnp.minimum(face_cycle, 0.0) * padded[..., 1:-1, 1:]
    )
    return -(
        flux_radial[..., 1:, :]
        - flux_radial[..., :-1, :]
        + (flux_cycle[..., 1:] - flux_cycle[..., :-1])
    )


def rim_each(values):
    wrapped = with_halo(values, (("az", 3),), 1, True)
    return with_halo(wrapped, (("rad", 2),), 1, False)


def on_device(fluid_state, velocity, shifts, fraction):
    fields = fluid_state.shape[0]
    joined = jnp.concatenate([fluid_state, velocity], axis=0)
    padded = rim_each(joined)
    velocity_pad = padded[fields:]
    current = fluid_state
    current_pad = padded[:fields]
    for sweep_index in range(STEPS):
        if sweep_index > 0:
            current_pad = rim_each(current)
        sectioned = current + tendency(current_pad, velocity_pad)
        current = 0.5 * (current + (sectioned + tendency(rim_each(sectioned), velocity_pad)))
    block_width = fluid_state.shape[3]
    edge_width = block_width // 4 + 1
    largest = block_width + block_width // 4
    preceding = shifted(current, "az", 1)
    distant = shifted(current, "az", 2)[..., block_width - edge_width :]
    bit_count = largest.bit_length()
    spare = (1 << bit_count) - 1 - largest
    pieces = [distant, preceding, current]
    pieces.append(jnp.zeros(current.shape[:3] + (spare,), current.dtype))
    window = jnp.concatenate(pieces, axis=3)
    offset = largest - shifts
    for level in range(bit_count - 1, -1, -1):
        step_size = 1 << level
        length = window.shape[3]
        chosen = offset >> level & 1 == 1
        window = jnp.where(
            chosen[None, None, :, None], window[..., step_size:], window[..., : length - step_size]
        )
    trailing = window[..., :block_width]
    leading = window[..., 1 : block_width + 1]
    weight = fraction[None, None, :, None]
    return (1.0 - weight) * leading + weight * trailing


def solution(mesh):
    return jax.shard_map(
        on_device,
        mesh=mesh,
        in_specs=(P(None, None, "rad", "az"), P(None, None, "rad", "az"), P("rad"), P("rad")),
        out_specs=P(None, None, "rad", "az"),
        check_vma=False,
    )
```

profile of v0, /device:TPU:0, one launch (start us, length us, event | category | flops | bytes accessed | tf_op | source)
XLA Modules:
  0.0 97.3 jit_solution(17816492942951533789)
XLA Ops:
  0.0 1.0 %constant_dynamic-update-slice_fusion.1 = f32[7,2,64,128]{3,2,1,0:T(8,128)S(1)} fusion(f32[5,2,64,128]{3,2,1,0:T(8,128)} %param.4), kind=kLoop, calls=%fused_computation.116 | loop fusion | bytes 655360
  1.1 0.2 fusion.40
  1.3 0.5 collective-permute-start
  1.8 5.1 %collective-permute-start.1 = (f32[7,2,64,1]{3,2,1,0:T(8,128)S(1)}, f32[7,2,64,1]{3,2,1,0:T(8,128)S(1)}, u32[]{:S(2)}, u32[]{:S(2)}) collective-permute-start(f32[7,2,64,1]{3,2,1,0:T(8,128)S(1)} %get-tuple-element.16), channel_id=1, source_target_pairs={{2,0},{4,2},{6,4},{8,6},{10,8},{12,10},{14,12},{16,14},{18,16},{20... | collective-permute-start | bytes 10760 | tf_op jit(solution)/shard_map/ppermute | solution.py:17
  6.8 6.2 %collective-permute-done = f32[7,2,64,1]{3,2,1,0:T(8,128)S(1)} collective-permute-done((f32[7,2,64,1]{3,2,1,0:T(8,128)S(1)}, f32[7,2,64,1]{3,2,1,0:T(8,128)S(1)}, u32[]{:S(2)}, u32[]{:S(2)}) %collective-permute-start) | collective-permute-done | bytes 3616 | tf_op jit(solution)/shard_map/ppermute | solution.py:16
  13.0 0.2 pad_maximum_fusion.35
  13.2 3.8 %collective-permute-start.2 = (f32[7,2,1,130]{3,2,1,0:T(1,128)S(1)}, f32[7,2,1,130]{3,2,1,0:T(1,128)S(1)}, u32[]{:S(2)}, u32[]{:S(2)}) collective-permute-start(f32[7,2,1,130]{3,2,1,0:T(1,128)S(1)} %get-tuple-element.7), channel_id=1, source_target_pairs={{0,1},{2,3},{4,5},{6,7},{8,9},{10,11},{12,13},{14,15},{16,17},{18,... | collective-permute-start | bytes 21848 | tf_op jit(solution)/shard_map/ppermute | solution.py:16
  17.0 1.3 %collective-permute-start.3 = (f32[7,2,1,130]{3,2,1,0:T(1,128)S(1)}, f32[7,2,1,130]{3,2,1,0:T(1,128)S(1)}, u32[]{:S(2)}, u32[]{:S(2)}) collective-permute-start(f32[7,2,1,130]{3,2,1,0:T(1,128)S(1)} %get-tuple-element.8), channel_id=1, source_target_pairs={{1,0},{3,2},{5,4},{7,6},{9,8},{11,10},{13,12},{15,14},{17,16},{19,... | collective-permute-start | bytes 21848 | tf_op jit(solution)/shard_map/ppermute | solution.py:17
  18.3 0.1 collective-permute-done.2
  18.4 4.2 %collective-permute-done.3 = f32[7,2,1,130]{3,2,1,0:T(1,128)S(1)} collective-permute-done((f32[7,2,1,130]{3,2,1,0:T(1,128)S(1)}, f32[7,2,1,130]{3,2,1,0:T(1,128)S(1)}, u32[]{:S(2)}, u32[]{:S(2)}) %collective-permute-start.3) | collective-permute-done | bytes 7312 | tf_op jit(solution)/shard_map/ppermute | solution.py:17
  22.6 0.2 maximum_bitcast_fusion
  22.8 0.1 broadcast_maximum_fusion.1
  22.9 0.1 broadcast_maximum_fusion
  23.0 0.3 fusion.18
  23.3 0.2 fusion.3
  23.6 0.7 copy-done
  24.3 0.2 fusion.36
  24.5 0.2 fusion.43
  24.6 2.4 %collective-permute-start.4 = (f32[5,2,64,1]{3,2,1,0:T(8,128)S(1)}, f32[5,2,64,1]{3,2,1,0:T(8,128)S(1)}, u32[]{:S(2)}, u32[]{:S(2)}) collective-permute-start(f32[5,2,64,1]{3,2,1,0:T(8,128)S(1)} %get-tuple-element.22), channel_id=1, source_target_pairs={{0,2},{2,4},{4,6},{6,8},{8,10},{10,12},{12,14},{14,16},{16,18},{18... | collective-permute-start | bytes 7688 | tf_op jit(solution)/shard_map/ppermute | solution.py:16
  27.0 2.1 %collective-permute-start.5 = (f32[5,2,64,1]{3,2,1,0:T(8,128)S(1)}, f32[5,2,64,1]{3,2,1,0:T(8,128)S(1)}, u32[]{:S(2)}, u32[]{:S(2)}) collective-permute-start(f32[5,2,64,1]{3,2,1,0:T(8,128)S(1)} %get-tuple-element.21), channel_id=1, source_target_pairs={{2,0},{4,2},{6,4},{8,6},{10,8},{12,10},{14,12},{16,14},{18,16},{20... | collective-permute-start | bytes 7688 | tf_op jit(solution)/shard_map/ppermute | solution.py:17
  29.1 4.9 %collective-permute-done.4 = f32[5,2,64,1]{3,2,1,0:T(8,128)S(1)} collective-permute-done((f32[5,2,64,1]{3,2,1,0:T(8,128)S(1)}, f32[5,2,64,1]{3,2,1,0:T(8,128)S(1)}, u32[]{:S(2)}, u32[]{:S(2)}) %collective-permute-start.4) | collective-permute-done | bytes 2592 | tf_op jit(solution)/shard_map/ppermute | solution.py:16
  34.0 0.1 pad_maximum_fusion.44
  34.1 1.6 %collective-permute-start.6 = (f32[5,2,1,130]{3,2,1,0:T(1,128)S(1)}, f32[5,2,1,130]{3,2,1,0:T(1,128)S(1)}, u32[]{:S(2)}, u32[]{:S(2)}) collective-permute-start(f32[5,2,1,130]{3,2,1,0:T(1,128)S(1)} %get-tuple-element.13), channel_id=1, source_target_pairs={{0,1},{2,3},{4,5},{6,7},{8,9},{10,11},{12,13},{14,15},{16,17},{18,... | collective-permute-start | bytes 15608 | tf_op jit(solution)/shard_map/ppermute | solution.py:16
  35.8 1.3 %collective-permute-start.7 = (f32[5,2,1,130]{3,2,1,0:T(1,128)S(1)}, f32[5,2,1,130]{3,2,1,0:T(1,128)S(1)}, u32[]{:S(2)}, u32[]{:S(2)}) collective-permute-start(f32[5,2,1,130]{3,2,1,0:T(1,128)S(1)} %get-tuple-element.14), channel_id=1, source_target_pairs={{1,0},{3,2},{5,4},{7,6},{9,8},{11,10},{13,12},{15,14},{17,16},{19,... | collective-permute-start | bytes 15608 | tf_op jit(solution)/shard_map/ppermute | solution.py:17
  37.1 0.2 fusion.5
  37.3 4.0 %collective-permute-done.7 = f32[5,2,1,130]{3,2,1,0:T(1,128)S(1)} collective-permute-done((f32[5,2,1,130]{3,2,1,0:T(1,128)S(1)}, f32[5,2,1,130]{3,2,1,0:T(1,128)S(1)}, u32[]{:S(2)}, u32[]{:S(2)}) %collective-permute-start.7) | collective-permute-done | bytes 5232 | tf_op jit(solution)/shard_map/ppermute | solution.py:17
  41.3 0.3 fusion.15
  41.6 0.2 fusion.33
  41.8 0.2 fusion.42
  41.9 1.8 %collective-permute-start.8 = (f32[5,2,64,1]{3,2,1,0:T(8,128)S(1)}, f32[5,2,64,1]{3,2,1,0:T(8,128)S(1)}, u32[]{:S(2)}, u32[]{:S(2)}) collective-permute-start(f32[5,2,64,1]{3,2,1,0:T(8,128)S(1)} %get-tuple-element.20), channel_id=1, source_target_pairs={{0,2},{2,4},{4,6},{6,8},{8,10},{10,12},{12,14},{14,16},{16,18},{18... | collective-permute-start | bytes 7688 | tf_op jit(solution)/shard_map/ppermute | solution.py:16
  43.8 2.6 %collective-permute-start.9 = (f32[5,2,64,1]{3,2,1,0:T(8,128)S(1)}, f32[5,2,64,1]{3,2,1,0:T(8,128)S(1)}, u32[]{:S(2)}, u32[]{:S(2)}) collective-permute-start(f32[5,2,64,1]{3,2,1,0:T(8,128)S(1)} %get-tuple-element.19), channel_id=1, source_target_pairs={{2,0},{4,2},{6,4},{8,6},{10,8},{12,10},{14,12},{16,14},{18,16},{20... | collective-permute-start | bytes 7688 | tf_op jit(solution)/shard_map/ppermute | solution.py:17
  46.4 4.9 %collective-permute-done.8 = f32[5,2,64,1]{3,2,1,0:T(8,128)S(1)} collective-permute-done((f32[5,2,64,1]{3,2,1,0:T(8,128)S(1)}, f32[5,2,64,1]{3,2,1,0:T(8,128)S(1)}, u32[]{:S(2)}, u32[]{:S(2)}) %collective-permute-start.8) | collective-permute-done | bytes 2592 | tf_op jit(solution)/shard_map/ppermute | solution.py:16
  51.3 0.1 pad_maximum_fusion.41
  51.4 1.6 %collective-permute-start.10 = (f32[5,2,1,130]{3,2,1,0:T(1,128)S(1)}, f32[5,2,1,130]{3,2,1,0:T(1,128)S(1)}, u32[]{:S(2)}, u32[]{:S(2)}) collective-permute-start(f32[5,2,1,130]{3,2,1,0:T(1,128)S(1)} %get-tuple-element.11), channel_id=1, source_target_pairs={{0,1},{2,3},{4,5},{6,7},{8,9},{10,11},{12,13},{14,15},{16,17},{18,... | collective-permute-start | bytes 15608 | tf_op jit(solution)/shard_map/ppermute | solution.py:16
  53.1 1.3 %collective-permute-start.11 = (f32[5,2,1,130]{3,2,1,0:T(1,128)S(1)}, f32[5,2,1,130]{3,2,1,0:T(1,128)S(1)}, u32[]{:S(2)}, u32[]{:S(2)}) collective-permute-start(f32[5,2,1,130]{3,2,1,0:T(1,128)S(1)} %get-tuple-element.12), channel_id=1, source_target_pairs={{1,0},{3,2},{5,4},{7,6},{9,8},{11,10},{13,12},{15,14},{17,16},{19,... | collective-permute-start | bytes 15608 | tf_op jit(solution)/shard_map/ppermute | solution.py:17
  54.4 0.2 fusion.6
  54.6 4.0 %collective-permute-done.11 = f32[5,2,1,130]{3,2,1,0:T(1,128)S(1)} collective-permute-done((f32[5,2,1,130]{3,2,1,0:T(1,128)S(1)}, f32[5,2,1,130]{3,2,1,0:T(1,128)S(1)}, u32[]{:S(2)}, u32[]{:S(2)}) %collective-permute-start.11) | collective-permute-done | bytes 5232 | tf_op jit(solution)/shard_map/ppermute | solution.py:17
  58.6 0.3 fusion.12
  58.9 0.2 fusion.28
  59.1 0.2 fusion.41
  59.3 1.8 %collective-permute-start.12 = (f32[5,2,64,1]{3,2,1,0:T(8,128)S(1)}, f32[5,2,64,1]{3,2,1,0:T(8,128)S(1)}, u32[]{:S(2)}, u32[]{:S(2)}) collective-permute-start(f32[5,2,64,1]{3,2,1,0:T(8,128)S(1)} %get-tuple-element.18), channel_id=1, source_target_pairs={{0,2},{2,4},{4,6},{6,8},{8,10},{10,12},{12,14},{14,16},{16,18},{18... | collective-permute-start | bytes 7688 | tf_op jit(solution)/shard_map/ppermute | solution.py:16
  61.1 2.6 %collective-permute-start.13 = (f32[5,2,64,1]{3,2,1,0:T(8,128)S(1)}, f32[5,2,64,1]{3,2,1,0:T(8,128)S(1)}, u32[]{:S(2)}, u32[]{:S(2)}) collective-permute-start(f32[5,2,64,1]{3,2,1,0:T(8,128)S(1)} %get-tuple-element.17), channel_id=1, source_target_pairs={{2,0},{4,2},{6,4},{8,6},{10,8},{12,10},{14,12},{16,14},{18,16},{20... | collective-permute-start | bytes 7688 | tf_op jit(solution)/shard_map/ppermute | solution.py:17
  63.8 4.9 %collective-permute-done.12 = f32[5,2,64,1]{3,2,1,0:T(8,128)S(1)} collective-permute-done((f32[5,2,64,1]{3,2,1,0:T(8,128)S(1)}, f32[5,2,64,1]{3,2,1,0:T(8,128)S(1)}, u32[]{:S(2)}, u32[]{:S(2)}) %collective-permute-start.12) | collective-permute-done | bytes 2592 | tf_op jit(solution)/shard_map/ppermute | solution.py:16
  68.6 0.1 pad_maximum_fusion.38
  68.7 1.6 %collective-permute-start.14 = (f32[5,2,1,130]{3,2,1,0:T(1,128)S(1)}, f32[5,2,1,130]{3,2,1,0:T(1,128)S(1)}, u32[]{:S(2)}, u32[]{:S(2)}) collective-permute-start(f32[5,2,1,130]{3,2,1,0:T(1,128)S(1)} %get-tuple-element.9), channel_id=1, source_target_pairs={{0,1},{2,3},{4,5},{6,7},{8,9},{10,11},{12,13},{14,15},{16,17},{18,... | collective-permute-start | bytes 15608 | tf_op jit(solution)/shard_map/ppermute | solution.py:16
  70.4 1.3 %collective-permute-start.15 = (f32[5,2,1,130]{3,2,1,0:T(1,128)S(1)}, f32[5,2,1,130]{3,2,1,0:T(1,128)S(1)}, u32[]{:S(2)}, u32[]{:S(2)}) collective-permute-start(f32[5,2,1,130]{3,2,1,0:T(1,128)S(1)} %get-tuple-element.10), channel_id=1, source_target_pairs={{1,0},{3,2},{5,4},{7,6},{9,8},{11,10},{13,12},{15,14},{17,16},{19,... | collective-permute-start | bytes 15608 | tf_op jit(solution)/shard_map/ppermute | solution.py:17
  71.7 0.2 fusion.7
  72.0 4.0 %collective-permute-done.15 = f32[5,2,1,130]{3,2,1,0:T(1,128)S(1)} collective-permute-done((f32[5,2,1,130]{3,2,1,0:T(1,128)S(1)}, f32[5,2,1,130]{3,2,1,0:T(1,128)S(1)}, u32[]{:S(2)}, u32[]{:S(2)}) %collective-permute-start.15) | collective-permute-done | bytes 5232 | tf_op jit(solution)/shard_map/ppermute | solution.py:17
  76.0 0.3 fusion.9
  76.2 0.2 fusion.25
  76.4 3.0 %collective-permute-start.17 = (f32[5,2,64,128]{3,2,1,0:T(8,128)S(1)}, f32[5,2,64,128]{3,2,1,0:T(8,128)S(1)}, u32[]{:S(2)}, u32[]{:S(2)}) collective-permute-start(f32[5,2,64,128]{3,2,1,0:T(8,128)S(1)} %fusion.25), channel_id=1, source_target_pairs={{0,4},{2,6},{4,8},{6,10},{8,12},{10,14},{12,16},{14,18},{16,20},{1... | collective-permute-start | bytes 983048 | tf_op jit(solution)/shard_map/ppermute | solution.py:25
  79.5 0.6 copy-done.3
  80.1 13.4 %collective-permute-done.17 = f32[5,2,64,128]{3,2,1,0:T(8,128)S(1)} collective-permute-done((f32[5,2,64,128]{3,2,1,0:T(8,128)S(1)}, f32[5,2,64,128]{3,2,1,0:T(8,128)S(1)}, u32[]{:S(2)}, u32[]{:S(2)}) %collective-permute-start.17) | collective-permute-done | bytes 327712 | tf_op jit(solution)/shard_map/ppermute | solution.py:25
  93.5 0.1 slice.349
  93.7 0.4 collective-permute-done.16
  94.1 0.6 fusion
  94.7 0.2 slice_select_fusion.6
  94.9 0.2 slice_select_fusion.5
  95.2 0.2 slice_select_fusion.4
  95.4 0.2 slice_select_fusion.3
  95.7 0.2 slice_select_fusion.2
  95.9 0.2 slice_select_fusion.1
  96.2 0.2 slice_select_fusion
  96.4 0.9 fusion.20
  (19 shorter events, 0.1 us)
Async XLA Ops:
  0.0 1.0 %copy-start.1 = (f32[2,2,64,128]{3,2,1,0:T(8,128)S(1)}, f32[2,2,64,128]{3,2,1,0:T(8,128)}, u32[]{:S(2)}) copy-start(f32[2,2,64,128]{3,2,1,0:T(8,128)} %param.5) | copy-start | bytes 393220
  1.3 11.8 %collective-permute-start = (f32[7,2,64,1]{3,2,1,0:T(8,128)S(1)}, f32[7,2,64,1]{3,2,1,0:T(8,128)S(1)}, u32[]{:S(2)}, u32[]{:S(2)}) collective-permute-start(f32[7,2,64,1]{3,2,1,0:T(8,128)S(1)} %get-tuple-element.15), channel_id=1, source_target_pairs={{0,2},{2,4},{4,6},{6,8},{8,10},{10,12},{12,14},{14,16},{16,18},{18... | collective-permute-start | bytes 10760 | tf_op jit(solution)/shard_map/ppermute | solution.py:16
  1.8 11.3 %collective-permute-start.1 = (f32[7,2,64,1]{3,2,1,0:T(8,128)S(1)}, f32[7,2,64,1]{3,2,1,0:T(8,128)S(1)}, u32[]{:S(2)}, u32[]{:S(2)}) collective-permute-start(f32[7,2,64,1]{3,2,1,0:T(8,128)S(1)} %get-tuple-element.16), channel_id=1, source_target_pairs={{2,0},{4,2},{6,4},{8,6},{10,8},{12,10},{14,12},{16,14},{18,16},{20... | collective-permute-start | bytes 10760 | tf_op jit(solution)/shard_map/ppermute | solution.py:17
  13.2 5.2 %collective-permute-start.2 = (f32[7,2,1,130]{3,2,1,0:T(1,128)S(1)}, f32[7,2,1,130]{3,2,1,0:T(1,128)S(1)}, u32[]{:S(2)}, u32[]{:S(2)}) collective-permute-start(f32[7,2,1,130]{3,2,1,0:T(1,128)S(1)} %get-tuple-element.7), channel_id=1, source_target_pairs={{0,1},{2,3},{4,5},{6,7},{8,9},{10,11},{12,13},{14,15},{16,17},{18,... | collective-permute-start | bytes 21848 | tf_op jit(solution)/shard_map/ppermute | solution.py:16
  17.0 5.6 %collective-permute-start.3 = (f32[7,2,1,130]{3,2,1,0:T(1,128)S(1)}, f32[7,2,1,130]{3,2,1,0:T(1,128)S(1)}, u32[]{:S(2)}, u32[]{:S(2)}) collective-permute-start(f32[7,2,1,130]{3,2,1,0:T(1,128)S(1)} %get-tuple-element.8), channel_id=1, source_target_pairs={{1,0},{3,2},{5,4},{7,6},{9,8},{11,10},{13,12},{15,14},{17,16},{19,... | collective-permute-start | bytes 21848 | tf_op jit(solution)/shard_map/ppermute | solution.py:17
  23.3 1.0 %copy-start = (f32[5,2,64,128]{3,2,1,0:T(8,128)S(1)}, f32[5,2,64,128]{3,2,1,0:T(8,128)}, u32[]{:S(2)}) copy-start(f32[5,2,64,128]{3,2,1,0:T(8,128)} %param.4) | copy-start | bytes 983044
  24.6 9.4 %collective-permute-start.4 = (f32[5,2,64,1]{3,2,1,0:T(8,128)S(1)}, f32[5,2,64,1]{3,2,1,0:T(8,128)S(1)}, u32[]{:S(2)}, u32[]{:S(2)}) collective-permute-start(f32[5,2,64,1]{3,2,1,0:T(8,128)S(1)} %get-tuple-element.22), channel_id=1, source_target_pairs={{0,2},{2,4},{4,6},{6,8},{8,10},{10,12},{12,14},{14,16},{16,18},{18... | collective-permute-start | bytes 7688 | tf_op jit(solution)/shard_map/ppermute | solution.py:16
  27.0 7.0 %collective-permute-start.5 = (f32[5,2,64,1]{3,2,1,0:T(8,128)S(1)}, f32[5,2,64,1]{3,2,1,0:T(8,128)S(1)}, u32[]{:S(2)}, u32[]{:S(2)}) collective-permute-start(f32[5,2,64,1]{3,2,1,0:T(8,128)S(1)} %get-tuple-element.21), channel_id=1, source_target_pairs={{2,0},{4,2},{6,4},{8,6},{10,8},{12,10},{14,12},{16,14},{18,16},{20... | collective-permute-start | bytes 7688 | tf_op jit(solution)/shard_map/ppermute | solution.py:17
  34.1 3.2 %collective-permute-start.6 = (f32[5,2,1,130]{3,2,1,0:T(1,128)S(1)}, f32[5,2,1,130]{3,2,1,0:T(1,128)S(1)}, u32[]{:S(2)}, u32[]{:S(2)}) collective-permute-start(f32[5,2,1,130]{3,2,1,0:T(1,128)S(1)} %get-tuple-element.13), channel_id=1, source_target_pairs={{0,1},{2,3},{4,5},{6,7},{8,9},{10,11},{12,13},{14,15},{16,17},{18,... | collective-permute-start | bytes 15608 | tf_op jit(solution)/shard_map/ppermute | solution.py:16
  35.8 5.6 %collective-permute-start.7 = (f32[5,2,1,130]{3,2,1,0:T(1,128)S(1)}, f32[5,2,1,130]{3,2,1,0:T(1,128)S(1)}, u32[]{:S(2)}, u32[]{:S(2)}) collective-permute-start(f32[5,2,1,130]{3,2,1,0:T(1,128)S(1)} %get-tuple-element.14), channel_id=1, source_target_pairs={{1,0},{3,2},{5,4},{7,6},{9,8},{11,10},{13,12},{15,14},{17,16},{19,... | collective-permute-start | bytes 15608 | tf_op jit(solution)/shard_map/ppermute | solution.py:17
  41.9 9.4 %collective-permute-start.8 = (f32[5,2,64,1]{3,2,1,0:T(8,128)S(1)}, f32[5,2,64,1]{3,2,1,0:T(8,128)S(1)}, u32[]{:S(2)}, u32[]{:S(2)}) collective-permute-start(f32[5,2,64,1]{3,2,1,0:T(8,128)S(1)} %get-tuple-element.20), channel_id=1, source_target_pairs={{0,2},{2,4},{4,6},{6,8},{8,10},{10,12},{12,14},{14,16},{16,18},{18... | collective-permute-start | bytes 7688 | tf_op jit(solution)/shard_map/ppermute | solution.py:16
  43.8 7.5 %collective-permute-start.9 = (f32[5,2,64,1]{3,2,1,0:T(8,128)S(1)}, f32[5,2,64,1]{3,2,1,0:T(8,128)S(1)}, u32[]{:S(2)}, u32[]{:S(2)}) collective-permute-start(f32[5,2,64,1]{3,2,1,0:T(8,128)S(1)} %get-tuple-element.19), channel_id=1, source_target_pairs={{2,0},{4,2},{6,4},{8,6},{10,8},{12,10},{14,12},{16,14},{18,16},{20... | collective-permute-start | bytes 7688 | tf_op jit(solution)/shard_map/ppermute | solution.py:17
  51.4 3.2 %collective-permute-start.10 = (f32[5,2,1,130]{3,2,1,0:T(1,128)S(1)}, f32[5,2,1,130]{3,2,1,0:T(1,128)S(1)}, u32[]{:S(2)}, u32[]{:S(2)}) collective-permute-start(f32[5,2,1,130]{3,2,1,0:T(1,128)S(1)} %get-tuple-element.11), channel_id=1, source_target_pairs={{0,1},{2,3},{4,5},{6,7},{8,9},{10,11},{12,13},{14,15},{16,17},{18,... | collective-permute-start | bytes 15608 | tf_op jit(solution)/shard_map/ppermute | solution.py:16
  53.1 5.6 %collective-permute-start.11 = (f32[5,2,1,130]{3,2,1,0:T(1,128)S(1)}, f32[5,2,1,130]{3,2,1,0:T(1,128)S(1)}, u32[]{:S(2)}, u32[]{:S(2)}) collective-permute-start(f32[5,2,1,130]{3,2,1,0:T(1,128)S(1)} %get-tuple-element.12), channel_id=1, source_target_pairs={{1,0},{3,2},{5,4},{7,6},{9,8},{11,10},{13,12},{15,14},{17,16},{19,... | collective-permute-start | bytes 15608 | tf_op jit(solution)/shard_map/ppermute | solution.py:17
  59.2 4.5 %copy-start.2 = (f32[64]{0:T(128)S(1)}, f32[64]{0:T(128)}, u32[]{:S(2)}) copy-start(f32[64]{0:T(128)} %param.7) | copy-start | bytes 772
  59.3 9.4 %collective-permute-start.12 = (f32[5,2,64,1]{3,2,1,0:T(8,128)S(1)}, f32[5,2,64,1]{3,2,1,0:T(8,128)S(1)}, u32[]{:S(2)}, u32[]{:S(2)}) collective-permute-start(f32[5,2,64,1]{3,2,1,0:T(8,128)S(1)} %get-tuple-element.18), channel_id=1, source_target_pairs={{0,2},{2,4},{4,6},{6,8},{8,10},{10,12},{12,14},{14,16},{16,18},{18... | collective-permute-start | bytes 7688 | tf_op jit(solution)/shard_map/ppermute | solution.py:16
  61.1 7.5 %collective-permute-start.13 = (f32[5,2,64,1]{3,2,1,0:T(8,128)S(1)}, f32[5,2,64,1]{3,2,1,0:T(8,128)S(1)}, u32[]{:S(2)}, u32[]{:S(2)}) collective-permute-start(f32[5,2,64,1]{3,2,1,0:T(8,128)S(1)} %get-tuple-element.17), channel_id=1, source_target_pairs={{2,0},{4,2},{6,4},{8,6},{10,8},{12,10},{14,12},{16,14},{18,16},{20... | collective-permute-start | bytes 7688 | tf_op jit(solution)/shard_map/ppermute | solution.py:17
  68.7 3.2 %collective-permute-start.14 = (f32[5,2,1,130]{3,2,1,0:T(1,128)S(1)}, f32[5,2,1,130]{3,2,1,0:T(1,128)S(1)}, u32[]{:S(2)}, u32[]{:S(2)}) collective-permute-start(f32[5,2,1,130]{3,2,1,0:T(1,128)S(1)} %get-tuple-element.9), channel_id=1, source_target_pairs={{0,1},{2,3},{4,5},{6,7},{8,9},{10,11},{12,13},{14,15},{16,17},{18,... | collective-permute-start | bytes 15608 | tf_op jit(solution)/shard_map/ppermute | solution.py:16
  70.4 5.6 %collective-permute-start.15 = (f32[5,2,1,130]{3,2,1,0:T(1,128)S(1)}, f32[5,2,1,130]{3,2,1,0:T(1,128)S(1)}, u32[]{:S(2)}, u32[]{:S(2)}) collective-permute-start(f32[5,2,1,130]{3,2,1,0:T(1,128)S(1)} %get-tuple-element.10), channel_id=1, source_target_pairs={{1,0},{3,2},{5,4},{7,6},{9,8},{11,10},{13,12},{15,14},{17,16},{19,... | collective-permute-start | bytes 15608 | tf_op jit(solution)/shard_map/ppermute | solution.py:17
  76.4 17.1 %collective-permute-start.17 = (f32[5,2,64,128]{3,2,1,0:T(8,128)S(1)}, f32[5,2,64,128]{3,2,1,0:T(8,128)S(1)}, u32[]{:S(2)}, u32[]{:S(2)}) collective-permute-start(f32[5,2,64,128]{3,2,1,0:T(8,128)S(1)} %fusion.25), channel_id=1, source_target_pairs={{0,4},{2,6},{4,8},{6,10},{8,12},{10,14},{12,16},{14,18},{16,20},{1... | collective-permute-start | bytes 983048 | tf_op jit(solution)/shard_map/ppermute | solution.py:25
  79.4 14.7 %collective-permute-start.16 = (f32[5,2,64,128]{3,2,1,0:T(8,128)S(1)}, f32[5,2,64,128]{3,2,1,0:T(8,128)S(1)}, u32[]{:S(2)}, u32[]{:S(2)}) collective-permute-start(f32[5,2,64,128]{3,2,1,0:T(8,128)S(1)} %fusion.25), channel_id=1, source_target_pairs={{0,2},{2,4},{4,6},{6,8},{8,10},{10,12},{12,14},{14,16},{16,18},{18... | collective-permute-start | bytes 983048 | tf_op jit(solution)/shard_map/ppermute | solution.py:25
  79.4 0.7 copy-start.3
where the time goes:
time: 97.7 us; the launch traced here: 97.3 us
  waiting for transfers between devices  51 us (52%)
  starting transfers between devices  36 us (37%)
  other arithmetic  6.84 us (7%)
  local copies, waits for them, and re-layouts  3.23 us (3%)
    ppermute x8, waiting for transfers between devices, with_halo(): before = lax.ppermute(last, axis, up)  20.9 us
    ppermute x8, starting transfers between devices, with_halo(): after = lax.ppermute(first, axis, down)  17.7 us
    ppermute x8, waiting for transfers between devices, with_halo(): after = lax.ppermute(first, axis, down)  16.2 us
    ppermute x8, starting transfers between devices, with_halo(): before = lax.ppermute(last, axis, up)  15.3 us
    ppermute x2, waiting for transfers between devices, shifted(): return lax.ppermute(value, axis, pairs)  13.8 us
    ppermute x2, starting transfers between devices, shifted(): return lax.ppermute(value, axis, pairs)  3 us
    unnamed x9, local copies, waits for them, and re-layouts  2.33 us
    select_n x8, other arithmetic, on_device(): jnp.where(chosen[None, None, :, None], window[..., step_size:], window[.....  2.29 us
  transfers between devices with their start and end apart: 18, of which 11 were waited for; matrix products, arithmetic and copies ran while one was open for 1% of the time, Pallas kernels for 0%

commit v1 on v0

v1 whole, which is shorter than its diff:
```python
import functools

import jax
import jax.numpy as jnp
from jax import lax
from jax.experimental import pallas as pl
from jax.experimental.pallas import tpu as pltpu
from jax.sharding import PartitionSpec as P

STEPS = 2
EDGE = 8


def kernel(
    n_az, n_rad, fields, layers,
    fluid, vel, shift_ref, frac_ref, out,
    xin, edge_lo, edge_hi, row_lo, row_hi, halo_l, halo_r, halo_d, halo_u,
    coef, rot, tail, got, got_tail, done,
    in_sem, send_h, recv_h, send_a, recv_a, send_b, recv_b, out_sem,
):
    slabs = fields * layers
    vels = 2 * layers
    total = slabs + vels
    rows, width = xin.shape[1], xin.shape[2]
    tall = rows + 2 * EDGE
    az = lax.axis_index("az")
    rad = lax.axis_index("rad")
    right = lax.rem(az + 1, n_az)
    right2 = lax.rem(az + 2, n_az)
    left = lax.rem(az + n_az - 1, n_az)
    left2 = lax.rem(az + n_az - 2, n_az)
    has_dn = rad > 0
    has_up = rad < n_rad - 1

    def dev(a, r):
        return {"az": a, "rad": r}

    load_f = pltpu.make_async_copy(fluid, xin.at[pl.ds(0, slabs)], in_sem.at[0])
    load_v = pltpu.make_async_copy(vel, xin.at[pl.ds(slabs, vels)], in_sem.at[1])
    load_f.start()
    load_v.start()

    barrier = pltpu.get_barrier_semaphore()
    for a in (left, right, left2):
        pl.semaphore_signal(barrier, inc=1, device_id=dev(a, rad))

    @pl.when(has_dn)
    def _():
        for a in (left, az, right):
            pl.semaphore_signal(barrier, inc=1, device_id=dev(a, rad - 1))

    @pl.when(has_up)
    def _():
        for a in (left, az, right):
            pl.semaphore_signal(barrier, inc=1, device_id=dev(a, rad + 1))

    sub8 = lax.broadcasted_iota(jnp.int32, (EDGE, width), 0)
    lane_r = lax.broadcasted_iota(jnp.int32, (rows, width), 1)
    row_r = lax.broadcasted_iota(jnp.int32, (rows, width), 0)
    lane_t = lax.broadcasted_iota(jnp.int32, (tall, width), 1)
    row_t = lax.broadcasted_iota(jnp.int32, (tall, 2 * width), 0)
    half = EDGE // 2

    pick = row_r[:, :rows] == lane_r[:, :rows]

    def to_rows(ref):
        spread = jnp.broadcast_to(ref[...].astype(jnp.float32), (rows, rows))
        return jnp.sum(jnp.where(pick, spread, 0.0), axis=1, keepdims=True)

    shift = jnp.broadcast_to(to_rows(shift_ref).astype(jnp.int32), (rows, width))
    weight = jnp.broadcast_to(to_rows(frac_ref), (rows, width))

    load_f.wait()
    load_v.wait()

    for i in range(total // 2):
        a, b = xin[2 * i, rows - EDGE :, :], xin[2 * i + 1, rows - EDGE :, :]
        row_hi[i] = jnp.where(sub8 >= half, a, pltpu.roll(b, half, 0))
        a, b = xin[2 * i, :EDGE, :], xin[2 * i + 1, :EDGE, :]
        row_lo[i] = jnp.where(sub8 < half, a, pltpu.roll(b, half, 0))
    hi = xin[0]
    lo = xin[0]
    hi = pltpu.roll(hi, EDGE, 1)
    for j in range(1, total):
        x = xin[j]
        mine = (lane_r >= EDGE * j) & (lane_r < EDGE * (j + 1))
        hi = jnp.where(mine, pltpu.roll(x, (EDGE * (j + 1)) % width, 1), hi)
        lo = jnp.where(mine, pltpu.roll(x, EDGE * j, 1), lo)
    edge_hi[...] = hi
    edge_lo[...] = lo

    pl.semaphore_wait(
        barrier, 3 + 3 * has_dn.astype(jnp.int32) + 3 * has_up.astype(jnp.int32)
    )

    def remote(src, dst, k, a, r):
        return pltpu.make_async_remote_copy(
            src_ref=src, dst_ref=dst, send_sem=send_h.at[k], recv_sem=recv_h.at[k],
            device_id=dev(a, r), device_id_type=pl.DeviceIdType.MESH,
        )

    top = pl.ds(rows - EDGE, EDGE)
    bottom = pl.ds(0, EDGE)
    mid = pl.ds(EDGE, rows)
    after = pl.ds(EDGE + rows, EDGE)
    before = pl.ds(0, EDGE)
    to_up = [
        remote(row_hi, halo_d, 2, az, rad + 1),
        remote(edge_hi.at[top], halo_l.at[before], 3, right, rad + 1),
        remote(edge_lo.at[top], halo_r.at[before], 4, left, rad + 1),
    ]
    to_dn = [
        remote(row_lo, halo_u, 5, az, rad - 1),
        remote(edge_hi.at[bottom], halo_l.at[after], 6, right, rad - 1),
        remote(edge_lo.at[bottom], halo_r.at[after], 7, left, rad - 1),
    ]
    sides = [
        remote(edge_hi, halo_l.at[mid], 0, right, rad),
        remote(edge_lo, halo_r.at[mid], 1, left, rad),
    ]
    for c in sides:
        c.start()

    @pl.when(has_up)
    def _():
        for c in to_up:
            c.start()

    @pl.when(has_dn)
    def _():
        for c in to_dn:
            c.start()

    for c in sides:
        c.wait()

    @pl.when(has_dn)
    def _():
        for c in to_up:
            c.wait_recv()
        for c in to_dn:
            c.wait_send()

    @pl.when(has_up)
    def _():
        for c in to_dn:
            c.wait_recv()
        for c in to_up:
            c.wait_send()

    inside = jnp.logical_and(
        jnp.logical_or(row_t >= EDGE, has_dn),
        jnp.logical_or(row_t < EDGE + rows, has_up),
    )

    def extended(j, pair, odd):
        below, above = halo_d[pair], halo_u[pair]
        below = jnp.where(odd, pltpu.roll(below, half, 0), below)
        above = jnp.where(odd, pltpu.roll(above, half, 0), above)
        own = jnp.concatenate([below, xin[j], above], axis=0)
        r = pltpu.roll(halo_r[...], width - EDGE * j, 1)
        l = pltpu.roll(halo_l[...], 2 * width - EDGE * (j + 1), 1)
        ext = jnp.where(lane_t < width // 2, r, l)
        whole = jnp.concatenate([own, ext], axis=1)
        return jnp.where(inside, whole, 0.0)

    def prev(x, axis):
        return pltpu.roll(x, 1, axis)

    def nxt(x, axis):
        return pltpu.roll(x, x.shape[axis] - 1, axis)

    for layer in range(layers):
        jr, ja = slabs + layer, slabs + layers + layer
        vr = extended(jr, jr // 2, jr % 2 == 1)
        va = extended(ja, ja // 2, ja % 2 == 1)
        face_r = 0.5 * (prev(vr, 0) + vr)
        face_a = 0.5 * (prev(va, 1) + va)
        rp, rm = jnp.maximum(face_r, 0.0), jnp.minimum(face_r, 0.0)
        ap, am = jnp.maximum(face_a, 0.0), jnp.minimum(face_a, 0.0)
        mid_c = 1.0 + ((rm - nxt(rp, 0)) + (am - nxt(ap, 1)))
        coef[layer, 0] = jnp.where(inside, mid_c, 0.0)
        coef[layer, 1] = jnp.where(inside, rp, 0.0)
        coef[layer, 2] = jnp.where(inside, -nxt(rm, 0), 0.0)
        coef[layer, 3] = jnp.where(inside, ap, 0.0)
        coef[layer, 4] = jnp.where(inside, -nxt(am, 1), 0.0)

    source = (lane_r - shift) & (width - 1)

    def send_a_of(j):
        return pltpu.make_async_remote_copy(
            src_ref=rot.at[j], dst_ref=got.at[j], send_sem=send_a.at[j], recv_sem=recv_a.at[j],
            device_id=dev(right, rad), device_id_type=pl.DeviceIdType.MESH,
        )

    def send_b_of(j):
        return pltpu.make_async_remote_copy(
            src_ref=tail.at[j], dst_ref=got_tail.at[j], send_sem=send_b.at[j], recv_sem=recv_b.at[j],
            device_id=dev(right2, rad), device_id_type=pl.DeviceIdType.MESH,
        )

    quarter = width // 4
    rows4 = rows // 4

    def slab_of(i):
        return lax.rem(i, fields) * layers + lax.div(i, fields), lax.div(i, fields)

    def work(i, carry):
        j, layer = slab_of(i)
        v = extended(j, lax.div(j, layers), layer == 1)

        def stencil(x):
            return (
                coef[layer, 0] * x
                + coef[layer, 1] * prev(x, 0)
                + coef[layer, 2] * nxt(x, 0)
                + coef[layer, 3] * prev(x, 1)
                + coef[layer, 4] * nxt(x, 1)
            )

        for _ in range(STEPS):
            v = 0.5 * (v + stencil(stencil(v)))
        lead = v[EDGE : EDGE + rows, :width]
        trail = prev(v, 1)[EDGE : EDGE + rows, :width]
        y = (1.0 - weight) * lead + weight * trail
        turned = jnp.take_along_axis(y, source, axis=1, mode="promise_in_bounds")
        rot[j] = turned
        send_a_of(j).start()
        packed = turned[:rows4]
        lane_q = lane_r[:rows4]
        for q in range(1, 4):
            part = pltpu.roll(turned[q * rows4 : (q + 1) * rows4], q * quarter, 1)
            packed = jnp.where(lane_q >= q * quarter, part, packed)
        tail[j] = packed
        send_b_of(j).start()
        return carry

    lax.fori_loop(0, slabs, work, 0)

    def out_of(j):
        return pltpu.make_async_copy(done.at[j], out.at[j], out_sem.at[j])

    def finish(i, carry):
        j, _ = slab_of(i)
        send_a_of(j).wait_recv()
        send_b_of(j).wait_recv()
        b = got_tail[j]
        parts = [b] + [pltpu.roll(b, width - q * quarter, 1) for q in range(1, 4)]
        far = jnp.concatenate(parts, axis=0)
        near = jnp.where(lane_r >= shift - width, got[j], far)
        done[j] = jnp.where(lane_r >= shift, rot[j], near)
        out_of(j).start()
        return carry

    lax.fori_loop(0, slabs, finish, 0)

    def drain(i, carry):
        j, _ = slab_of(i)
        send_a_of(j).wait_send()
        send_b_of(j).wait_send()
        out_of(j).wait()
        return carry

    lax.fori_loop(0, slabs, drain, 0)


def on_device(fluid_state, velocity, shifts, fraction):
    fields, layers, rows, width = fluid_state.shape
    n_az, n_rad = lax.axis_size("az"), lax.axis_size("rad")
    slabs, vels = fields * layers, 2 * layers
    total = slabs + vels
    tall = rows + 2 * EDGE
    f32 = jnp.float32
    dma = pltpu.SemaphoreType.DMA
    anywhere = pl.BlockSpec(memory_space=pl.ANY)
    vmem = pl.BlockSpec(memory_space=pltpu.VMEM)
    result = pl.pallas_call(
        functools.partial(kernel, n_az, n_rad, fields, layers),
        out_shape=jax.ShapeDtypeStruct((slabs, rows, width), f32),
        in_specs=[anywhere, anywhere, vmem, vmem],
        out_specs=anywhere,
        scratch_shapes=[
            pltpu.VMEM((total, rows, width), f32),
            pltpu.VMEM((rows, width), f32),
            pltpu.VMEM((rows, width), f32),
            pltpu.VMEM((total // 2, EDGE, width), f32),
            pltpu.VMEM((total // 2, EDGE, width), f32),
            pltpu.VMEM((tall, width), f32),
            pltpu.VMEM((tall, width), f32),
            pltpu.VMEM((total // 2, EDGE, width), f32),
            pltpu.VMEM((total // 2, EDGE, width), f32),
            pltpu.VMEM((layers, 5, tall, 2 * width), f32),
            pltpu.VMEM((slabs, rows, width), f32),
            pltpu.VMEM((slabs, rows // 4, width), f32),
            pltpu.VMEM((slabs, rows, width), f32),
            pltpu.VMEM((slabs, rows // 4, width), f32),
            pltpu.VMEM((slabs, rows, width), f32),
            dma((2,)), dma((8,)), dma((8,)),
            dma((slabs,)), dma((slabs,)), dma((slabs,)), dma((slabs,)), dma((slabs,)),
        ],
        compiler_params=pltpu.CompilerParams(
            collective_id=0, has_side_effects=True, vmem_limit_bytes=16 * 1024 * 1024
        ),
        cost_estimate=pl.CostEstimate(
            flops=50_000_000, bytes_accessed=800_000, transcendentals=0
        ),
    )(
        fluid_state.reshape(slabs, rows, width),
        velocity.reshape(vels, rows, width),
        shifts.reshape(1, rows),
        fraction.reshape(1, rows),
    )
    return result.reshape(fields, layers, rows, width)


def solution(mesh):
    return jax.shard_map(
        on_device,
        mesh=mesh,
        in_specs=(P(None, None, "rad", "az"), P(None, None, "rad", "az"), P("rad"), P("rad")),
        out_specs=P(None, None, "rad", "az"),
        check_vma=False,
    )
```

time: 97.7 us -> 25.4 us (0.26)
  waiting for transfers between devices: 51 us -> 0 us
  starting transfers between devices: 36 us -> 0 us
  Pallas kernels: 0 us -> 22 us
  other arithmetic: 6.84 us -> 0 us
    ppermute x18 -> x0, waiting for transfers between devices: 51 us -> none  [the longest x8 20.9 us: with_halo(): before = lax.ppermute(last, axis, up)]
    ppermute x18 -> x0, starting transfers between devices: 36 us -> none  [the longest x8 17.7 us: with_halo(): after = lax.ppermute(first, axis, down)]
    pallas_call x0 -> x1, Pallas kernels: none -> 22 us  [on_device(): pl.pallas_call(functools.partial(kernel, n_az, n_rad, fields, layers), ou...]
    add x11 -> x0, other arithmetic: 3.27 us -> none  [the longest x4 1.08 us: tendency(): jnp.maximum(face_radial, 0.0) * padded[..., :-1, 1:-1]]
    select_n x8 -> x0, other arithmetic: 2.29 us -> none  [on_device(): jnp.where(chosen[None, None, :, None], window[..., step_size:], window[.....]
  transfers between devices with their start and end apart: 18 -> 0, of which waited for: 11 -> 0; matrix products, arithmetic and copies ran while one was open for 1% -> 0% of each run, Pallas kernels for 0% -> 0%
where the time goes in v1:
time: 25.4 us; the launch traced here: 25.3 us
  Pallas kernels  22 us (87%)
  local copies, waits for them, and re-layouts  3.27 us (13%)
    pallas_call x1, Pallas kernels, on_device(): pl.pallas_call(functools.partial(kernel, n_az, n_rad, fields, layers), ou...  22 us
    unnamed x9, local copies, waits for them, and re-layouts  3.27 us

profile of v1, /device:TPU:0, one launch (start us, length us, event | category | flops | bytes accessed | tf_op | source)
XLA Modules:
  0.0 25.3 jit_solution(12155380656393583001)
XLA Ops:
  0.0 0.0 copy-start.2
  0.0 0.0 copy-start.3
  0.0 0.7 %copy-done.2 = s32[64]{0:T(128)S(1)} copy-done((s32[64]{0:T(128)S(1)}, s32[64]{0:T(128)}, u32[]{:S(2)}) %copy-start.2) | copy-done | bytes 280
  0.7 0.0 copy-done.3
  0.7 0.0 copy-start
  0.7 1.0 %copy-done = f32[5,2,64,128]{3,2,1,0:T(8,128)S(1)} copy-done((f32[5,2,64,128]{3,2,1,0:T(8,128)S(1)}, f32[5,2,64,128]{3,2,1,0:T(8,128)}, u32[]{:S(2)}) %copy-start) | copy-done | bytes 327704
  1.6 0.0 copy-start.1
  1.6 0.9 %copy-done.1 = f32[2,2,64,128]{3,2,1,0:T(8,128)S(1)} copy-done((f32[2,2,64,128]{3,2,1,0:T(8,128)S(1)}, f32[2,2,64,128]{3,2,1,0:T(8,128)}, u32[]{:S(2)}) %copy-start.1) | copy-done | bytes 131096
  2.5 22.0 %shard_map.46 = f32[10,64,128]{2,1,0:T(8,128)S(1)} custom-call(f32[10,64,128]{2,1,0:T(8,128)S(1)} %bitcast.6, f32[4,64,128]{2,1,0:T(8,128)S(1)} %bitcast.7, s32[1,64]{1,0:T(1,128)S(1)} %bitcast.8, f32[1,64]{1,0:T(1,128)S(1)} %bitcast.9), custom_call_target="tpu_custom_call" | custom-call | flops 50000000 | bytes 800000 | tf_op jit(solution)/shard_map/pallas_call | solution.py:277
  24.5 0.7 %copy.6 = f32[5,2,64,128]{3,2,1,0:T(8,128)} copy(f32[5,2,64,128]{3,2,1,0:T(8,128)S(1)} %bitcast.5) | data formatting | bytes 655360
Async XLA Ops:
  0.0 0.7 %copy-start.2 = (s32[64]{0:T(128)S(1)}, s32[64]{0:T(128)}, u32[]{:S(2)}) copy-start(s32[64]{0:T(128)} %param.6) | copy-start | bytes 772
  0.0 0.7 %copy-start.3 = (f32[64]{0:T(128)S(1)}, f32[64]{0:T(128)}, u32[]{:S(2)}) copy-start(f32[64]{0:T(128)} %param.7) | copy-start | bytes 772
  0.7 1.0 %copy-start = (f32[5,2,64,128]{3,2,1,0:T(8,128)S(1)}, f32[5,2,64,128]{3,2,1,0:T(8,128)}, u32[]{:S(2)}) copy-start(f32[5,2,64,128]{3,2,1,0:T(8,128)} %param.4) | copy-start | bytes 983044
  1.6 0.9 %copy-start.1 = (f32[2,2,64,128]{3,2,1,0:T(8,128)S(1)}, f32[2,2,64,128]{3,2,1,0:T(8,128)}, u32[]{:S(2)}) copy-start(f32[2,2,64,128]{3,2,1,0:T(8,128)} %param.5) | copy-start | bytes 393220

commit v2 on v1

v2 whole, which is shorter than its diff:
```python
import functools

import jax
import jax.numpy as jnp
from jax import lax
from jax.experimental import pallas as pl
from jax.experimental.pallas import tpu as pltpu
from jax.sharding import PartitionSpec as P

STEPS = 2
EDGE = 8
NINE = 9


def kernel(
    n_az, n_rad, fields, layers,
    fluid, vel, shift_hbm, frac_hbm, out,
    shift_ref, frac_ref, shift_b, weight_b, xin, own_lo, own_hi, row_lo, row_hi, halo_l, halo_r, halo_d, halo_u,
    coef, coef_s, coef_t, inner, rot, tail, got, got_tail,
    in_sem, send_h, recv_h, send_a, recv_a, send_b, recv_b,
):
    slabs = fields * layers
    vels = 2 * layers
    total = slabs + vels
    rows, width = xin.shape[1], xin.shape[2]
    tall = rows + 2 * EDGE
    az = lax.axis_index("az")
    rad = lax.axis_index("rad")
    right = lax.rem(az + 1, n_az)
    right2 = lax.rem(az + 2, n_az)
    left = lax.rem(az + n_az - 1, n_az)
    left2 = lax.rem(az + n_az - 2, n_az)
    has_dn = rad > 0
    has_up = rad < n_rad - 1

    def dev(a, r):
        return {"az": a, "rad": r}

    load_f = pltpu.make_async_copy(fluid, xin.at[pl.ds(0, slabs)], in_sem.at[0])
    load_v = pltpu.make_async_copy(vel, xin.at[pl.ds(slabs, vels)], in_sem.at[1])
    load_s = pltpu.make_async_copy(shift_hbm, shift_ref, in_sem.at[2])
    load_w = pltpu.make_async_copy(frac_hbm, frac_ref, in_sem.at[3])
    loads = (load_s, load_w, load_f, load_v)
    for c in loads:
        c.start()

    barrier = pltpu.get_barrier_semaphore()
    for a in (left, right, left2):
        pl.semaphore_signal(barrier, inc=1, device_id=dev(a, rad))

    @pl.when(has_dn)
    def _():
        for a in (left, az, right):
            pl.semaphore_signal(barrier, inc=1, device_id=dev(a, rad - 1))

    @pl.when(has_up)
    def _():
        for a in (left, az, right):
            pl.semaphore_signal(barrier, inc=1, device_id=dev(a, rad + 1))

    def iota(shape, axis):
        return lax.broadcasted_iota(jnp.int32, shape, axis)

    sub8 = iota((EDGE, width), 0)
    lane_r = iota((rows, width), 1)
    half = EDGE // 2
    own = pl.ds(EDGE, rows)

    for c in loads:
        c.wait()

    for i in range(total // 2):
        a, b = xin[2 * i, rows - EDGE :, :], xin[2 * i + 1, rows - EDGE :, :]
        row_hi[i] = jnp.where(sub8 >= half, a, pltpu.roll(b, half, 0))
        a, b = xin[2 * i, :EDGE, :], xin[2 * i + 1, :EDGE, :]
        row_lo[i] = jnp.where(sub8 < half, a, pltpu.roll(b, half, 0))
    lo = xin[0]
    hi = pltpu.roll(xin[0], NINE, 1)
    for j in range(1, total):
        x = xin[j]
        mine = lane_r >= NINE * j
        hi = jnp.where(mine, pltpu.roll(x, (NINE * (j + 1)) % width, 1), hi)
        lo = jnp.where(mine, pltpu.roll(x, NINE * j, 1), lo)
    own_hi[own, :] = hi
    own_lo[own, :] = lo

    def prev(x, axis):
        return pltpu.roll(x, 1, axis)

    def nxt(x, axis):
        return pltpu.roll(x, x.shape[axis] - 1, axis)

    def coefficients(vr, va, keep):
        face_r = 0.5 * (prev(vr, 0) + vr)
        face_a = 0.5 * (prev(va, 1) + va)
        rp, rm = jnp.maximum(face_r, 0.0), jnp.minimum(face_r, 0.0)
        ap, am = jnp.maximum(face_a, 0.0), jnp.minimum(face_a, 0.0)
        mid_c = 1.0 + ((rm - nxt(rp, 0)) + (am - nxt(ap, 1)))
        all5 = [mid_c, rp, -nxt(rm, 0), ap, -nxt(am, 1)]
        if keep is not None:
            all5 = [jnp.where(keep, c, 0.0) for c in all5]
        return all5

    def transport(values, pick):
        def stencil(n, x):
            return (
                (pick(n, 0) * x + pick(n, 1) * prev(x, 0))
                + (pick(n, 2) * nxt(x, 0) + pick(n, 3) * prev(x, 1))
                + pick(n, 4) * nxt(x, 1)
            )

        for _ in range(STEPS):
            once = [stencil(n, x) for n, x in enumerate(values)]
            twice = [stencil(n, x) for n, x in enumerate(once)]
            values = [0.5 * (x + t) for x, t in zip(values, twice)]
        return values

    for layer in range(layers):
        cs = coefficients(xin[slabs + layer], xin[slabs + layers + layer], None)
        for k in range(5):
            coef[layer, k] = cs[k]

    pick_row = iota((rows, rows), 0) == iota((rows, rows), 1)

    def to_rows(ref):
        spread = jnp.broadcast_to(ref[...].astype(jnp.float32), (rows, rows))
        return jnp.sum(jnp.where(pick_row, spread, 0.0), axis=1, keepdims=True)

    shift_b[...] = jnp.broadcast_to(to_rows(shift_ref).astype(jnp.int32), (rows, width))
    weight_b[...] = jnp.broadcast_to(to_rows(frac_ref), (rows, width))

    pl.semaphore_wait(
        barrier, 3 + 3 * has_dn.astype(jnp.int32) + 3 * has_up.astype(jnp.int32)
    )

    def remote(src, dst, k, a, r):
        return pltpu.make_async_remote_copy(
            src_ref=src, dst_ref=dst, send_sem=send_h.at[k], recv_sem=recv_h.at[k],
            device_id=dev(a, r), device_id_type=pl.DeviceIdType.MESH,
        )

    top = pl.ds(rows, EDGE)
    bottom = pl.ds(EDGE, EDGE)
    after = pl.ds(EDGE + rows, EDGE)
    before = pl.ds(0, EDGE)
    to_up = [
        remote(own_hi.at[top], halo_l.at[before], 3, right, rad + 1),
        remote(own_lo.at[top], halo_r.at[before], 4, left, rad + 1),
        remote(own_hi.at[top], own_hi.at[before], 8, az, rad + 1),
        remote(own_lo.at[top], own_lo.at[before], 9, az, rad + 1),
        remote(row_hi, halo_d, 2, az, rad + 1),
    ]
    to_dn = [
        remote(own_hi.at[bottom], halo_l.at[after], 6, right, rad - 1),
        remote(own_lo.at[bottom], halo_r.at[after], 7, left, rad - 1),
        remote(own_hi.at[bottom], own_hi.at[after], 10, az, rad - 1),
        remote(own_lo.at[bottom], own_lo.at[after], 11, az, rad - 1),
        remote(row_lo, halo_u, 5, az, rad - 1),
    ]
    sides = [
        remote(own_hi.at[own], halo_l.at[own], 0, right, rad),
        remote(own_lo.at[own], halo_r.at[own], 1, left, rad),
    ]
    for c in sides:
        c.start()

    @pl.when(has_up)
    def _():
        for c in to_up:
            c.start()

    @pl.when(has_dn)
    def _():
        for c in to_dn:
            c.start()

    def interior(layer, carry):
        values = [xin[f * layers + layer] for f in range(fields)]
        values = transport(values, lambda n, k: coef[layer, k])
        weight = weight_b[...]
        for f, v in enumerate(values):
            inner[f * layers + layer] = (1.0 - weight) * v + weight * prev(v, 1)
        return carry

    lax.fori_loop(0, layers, interior, 0)

    for c in sides:
        c.wait()

    @pl.when(has_dn)
    def _():
        for c in to_up:
            c.wait_recv()
        for c in to_dn:
            c.wait_send()

    @pl.when(has_up)
    def _():
        for c in to_dn:
            c.wait_recv()
        for c in to_up:
            c.wait_send()

    weight, shift = weight_b[...], shift_b[...]

    row_s = iota((4 * EDGE, width), 0)
    keep_s = jnp.logical_and(
        jnp.logical_or(row_s >= EDGE, has_dn), jnp.logical_or(row_s < 3 * EDGE, has_up)
    )

    def strip(j):
        below, above = halo_d[j // 2], halo_u[j // 2]
        if j % 2:
            below, above = pltpu.roll(below, half, 0), pltpu.roll(above, half, 0)
        both = jnp.concatenate([below, xin[j, :EDGE], xin[j, rows - EDGE :], above], axis=0)
        return jnp.where(keep_s, both, 0.0)

    for layer in range(layers):
        cs = coefficients(strip(slabs + layer), strip(slabs + layers + layer), keep_s)
        for k in range(5):
            coef_s[layer, k] = cs[k]

    lane_t = iota((tall, width), 1)
    row_t = iota((tall, width), 0)
    keep_t = jnp.logical_and(
        jnp.logical_or(row_t >= EDGE, has_dn), jnp.logical_or(row_t < EDGE + rows, has_up)
    )
    k16 = lane_t & 15
    group = lane_t >> 4
    on_right = (group & 1) == 1
    layer_of = (group >> 1) & 1
    part_of = group >> 2
    lag = NINE - 7
    offset = jnp.where(
        on_right,
        jnp.where(k16 < NINE, k16, k16 - NINE),
        jnp.where(k16 < 7, k16 + lag, k16 - 7),
    )
    use_l = jnp.logical_and(jnp.logical_not(on_right), k16 < 7)
    use_r = jnp.logical_and(on_right, k16 >= NINE)

    def take(x, index):
        return jnp.take_along_axis(x, index, axis=1, mode="promise_in_bounds")

    def columns(slab):
        index = NINE * slab + offset
        mine = jnp.where(on_right, take(own_hi[...], index), take(own_lo[...], index))
        x = jnp.where(use_l, take(halo_l[...], index), mine)
        x = jnp.where(use_r, take(halo_r[...], index), x)
        return jnp.where(keep_t, x, 0.0)

    cs = coefficients(
        columns(slabs + layer_of), columns(slabs + layers + layer_of), keep_t
    )
    for k in range(5):
        coef_t[k] = cs[k]

    tiles = (fields + 1) // 2
    cols = [
        columns(jnp.minimum(2 * t + part_of, fields - 1) * layers + layer_of)
        for t in range(tiles)
    ]
    cols = transport(cols, lambda n, k: coef_t[k])
    cols_y = []
    for v in cols:
        v, p = v[EDGE : EDGE + rows], prev(v, 1)[EDGE : EDGE + rows]
        cols_y.append((1.0 - weight) * v + weight * p)

    for layer in range(layers):
        js = [f * layers + layer for f in range(fields)]
        values = transport([strip(j) for j in js], lambda n, k: coef_s[layer, k])
        for j, v in zip(js, values):
            p = prev(v, 1)
            for lo_row, at, first in ((EDGE, 0, True), (2 * EDGE, rows - EDGE, False)):
                w = weight[at : at + EDGE]
                y = (1.0 - w) * v[lo_row : lo_row + EDGE] + w * p[lo_row : lo_row + EDGE]
                keep = sub8 < half if first else sub8 >= half
                inner[j, at : at + EDGE, :] = jnp.where(keep, y, inner[j, at : at + EDGE, :])

    source = (lane_r - shift) & (width - 1)
    in_strip = jnp.logical_or(source <= 4, source >= width - 4)
    strip_lane = jnp.where(source < width // 2, source + 7, source - (width - NINE) + 16)

    def send_a_of(j):
        return pltpu.make_async_remote_copy(
            src_ref=rot.at[j], dst_ref=got.at[j], send_sem=send_a.at[j], recv_sem=recv_a.at[j],
            device_id=dev(right, rad), device_id_type=pl.DeviceIdType.MESH,
        )

    def send_b_of(j):
        return pltpu.make_async_remote_copy(
            src_ref=tail.at[j], dst_ref=got_tail.at[j], send_sem=send_b.at[j], recv_sem=recv_b.at[j],
            device_id=dev(right2, rad), device_id_type=pl.DeviceIdType.MESH,
        )

    quarter = width // 4
    rows4 = rows // 4

    lane_q = lane_r[:rows4]
    for f in range(fields):
        for layer in range(layers):
            j = f * layers + layer
            at = (strip_lane + (64 * (f % 2) + 32 * layer)) & (width - 1)
            turned = jnp.where(in_strip, take(cols_y[f // 2], at), take(inner[j], source))
            rot[j] = turned
            send_a_of(j).start()
            packed = turned[:rows4]
            for q in range(1, 4):
                part = pltpu.roll(turned[q * rows4 : (q + 1) * rows4], q * quarter, 1)
                packed = jnp.where(lane_q >= q * quarter, part, packed)
            tail[j] = packed
            send_b_of(j).start()

    def finish(j, carry):
        send_a_of(j).wait_recv()
        send_b_of(j).wait_recv()
        b = got_tail[j]
        parts = [b] + [pltpu.roll(b, width - q * quarter, 1) for q in range(1, 4)]
        far = jnp.concatenate(parts, axis=0)
        near = jnp.where(lane_r >= shift - width, got[j], far)
        out[j] = jnp.where(lane_r >= shift, rot[j], near)
        return carry

    lax.fori_loop(0, slabs, finish, 0)

    def drain(j, carry):
        send_a_of(j).wait_send()
        send_b_of(j).wait_send()
        return carry

    lax.fori_loop(0, slabs, drain, 0)


def on_device(fluid_state, velocity, shifts, fraction):
    fields, layers, rows, width = fluid_state.shape
    n_az, n_rad = lax.axis_size("az"), lax.axis_size("rad")
    slabs, vels = fields * layers, 2 * layers
    total = slabs + vels
    tall = rows + 2 * EDGE
    f32 = jnp.float32
    dma = pltpu.SemaphoreType.DMA
    hbm = pl.BlockSpec(memory_space=pltpu.HBM)
    vmem = pl.BlockSpec(memory_space=pltpu.VMEM)
    result = pl.pallas_call(
        functools.partial(kernel, n_az, n_rad, fields, layers),
        out_shape=jax.ShapeDtypeStruct((slabs, rows, width), f32),
        in_specs=[hbm, hbm, hbm, hbm],
        out_specs=vmem,
        scratch_shapes=[
            pltpu.VMEM((1, rows), jnp.int32),
            pltpu.VMEM((1, rows), f32),
            pltpu.VMEM((rows, width), jnp.int32),
            pltpu.VMEM((rows, width), f32),
            pltpu.VMEM((total, rows, width), f32),
            pltpu.VMEM((tall, width), f32),
            pltpu.VMEM((tall, width), f32),
            pltpu.VMEM((total // 2, EDGE, width), f32),
            pltpu.VMEM((total // 2, EDGE, width), f32),
            pltpu.VMEM((tall, width), f32),
            pltpu.VMEM((tall, width), f32),
            pltpu.VMEM((total // 2, EDGE, width), f32),
            pltpu.VMEM((total // 2, EDGE, width), f32),
            pltpu.VMEM((layers, 5, rows, width), f32),
            pltpu.VMEM((layers, 5, 4 * EDGE, width), f32),
            pltpu.VMEM((5, tall, width), f32),
            pltpu.VMEM((slabs, rows, width), f32),
            pltpu.VMEM((slabs, rows, width), f32),
            pltpu.VMEM((slabs, rows // 4, width), f32),
            pltpu.VMEM((slabs, rows, width), f32),
            pltpu.VMEM((slabs, rows // 4, width), f32),
            dma((4,)), dma((12,)), dma((12,)),
            dma((slabs,)), dma((slabs,)), dma((slabs,)), dma((slabs,)),
        ],
        compiler_params=pltpu.CompilerParams(
            collective_id=0, has_side_effects=True, vmem_limit_bytes=60 * 1024 * 1024
        ),
        cost_estimate=pl.CostEstimate(
            flops=50_000_000, bytes_accessed=800_000, transcendentals=0
        ),
    )(
        fluid_state.reshape(slabs, rows, width),
        velocity.reshape(vels, rows, width),
        shifts.reshape(1, rows),
        fraction.reshape(1, rows),
    )
    return result.reshape(fields, layers, rows, width)


def solution(mesh):
    return jax.shard_map(
        on_device,
        mesh=mesh,
        in_specs=(P(None, None, "rad", "az"), P(None, None, "rad", "az"), P("rad"), P("rad")),
        out_specs=P(None, None, "rad", "az"),
        check_vma=False,
    )
```

time: 25.4 us -> 22.7 us (0.89)
  local copies, waits for them, and re-layouts: 3.27 us -> 1.72 us
  Pallas kernels: 22 us -> 20.8 us
    unnamed x9 -> x1, local copies, waits for them, and re-layouts: 3.27 us -> 1.72 us
    pallas_call x1, Pallas kernels: 22 us -> 20.8 us  [on_device(): pl.pallas_call(functools.partial(kernel, n_az, n_rad, fields, layers), ou...]
where the time goes in v2:
time: 22.7 us; the launch traced here: 22.6 us
  Pallas kernels  20.8 us (92%)
  local copies, waits for them, and re-layouts  1.72 us (8%)
    pallas_call x1, Pallas kernels, on_device(): pl.pallas_call(functools.partial(kernel, n_az, n_rad, fields, layers), ou...  20.8 us
    unnamed x1, local copies, waits for them, and re-layouts  1.72 us

profile of v2, /device:TPU:0, one launch (start us, length us, event | category | flops | bytes accessed | tf_op | source)
XLA Modules:
  0.0 22.6 jit_solution(10379764002386971719)
XLA Ops:
  0.0 20.8 %shard_map.46 = f32[10,64,128]{2,1,0:T(8,128)} custom-call(f32[10,64,128]{2,1,0:T(8,128)} %bitcast.6, f32[4,64,128]{2,1,0:T(8,128)} %bitcast.7, s32[1,64]{1,0:T(1,128)} %bitcast.8, f32[1,64]{1,0:T(1,128)} %bitcast.9), custom_call_target="tpu_custom_call" | custom-call | flops 50000000 | bytes 800000 | tf_op jit(solution)/shard_map/pallas_call | solution.py:344
  20.8 1.7 %copy.6 = f32[5,2,64,128]{3,2,1,0:T(8,128)} copy(f32[5,2,64,128]{3,2,1,0:T(8,128)} %bitcast.5) | data formatting | bytes 655360

commit v3 on v2

--- a/solution.py
+++ b/solution.py
@@ -16,7 +16,7 @@
     n_az, n_rad, fields, layers,
     fluid, vel, shift_hbm, frac_hbm, out,
     shift_ref, frac_ref, shift_b, weight_b, xin, own_lo, own_hi, row_lo, row_hi, halo_l, halo_r, halo_d, halo_u,
-    coef, coef_s, coef_t, inner, rot, tail, got, got_tail,
+    coef, coef_s, coef_t, seam, brim, got_brim, brim_tail, got_brim_tail, rot, tail, got, got_tail,
     in_sem, send_h, recv_h, send_a, recv_a, send_b, recv_b,
 ):
     slabs = fields * layers
@@ -57,6 +57,9 @@
     def _():
         for a in (left, az, right):
             pl.semaphore_signal(barrier, inc=1, device_id=dev(a, rad + 1))
+
+    quarter = width // 4
+    rows4 = rows // 4
 
     def iota(shape, axis):
         return lax.broadcasted_iota(jnp.int32, shape, axis)
@@ -174,12 +177,41 @@
         for c in to_dn:
             c.start()
 
+    def send_a_of(j):
+        return pltpu.make_async_remote_copy(
+            src_ref=rot.at[j], dst_ref=got.at[j], send_sem=send_a.at[j], recv_sem=recv_a.at[j],
+            device_id=dev(right, rad), device_id_type=pl.DeviceIdType.MESH,
+        )
+
+    def send_b_of(j):
+        return pltpu.make_async_remote_copy(
+            src_ref=tail.at[j], dst_ref=got_tail.at[j], send_sem=send_b.at[j], recv_sem=recv_b.at[j],
+            device_id=dev(right2, rad), device_id_type=pl.DeviceIdType.MESH,
+        )
+
+
+    def take(x, index):
+        return jnp.take_along_axis(x, index, axis=1, mode="promise_in_bounds")
+
+    weight, shift = weight_b[...], shift_b[...]
+    source = (lane_r - shift) & (width - 1)
+    lane_q = lane_r[:rows4]
+
     def interior(layer, carry):
         values = [xin[f * layers + layer] for f in range(fields)]
         values = transport(values, lambda n, k: coef[layer, k])
-        weight = weight_b[...]
         for f, v in enumerate(values):
-            inner[f * layers + layer] = (1.0 - weight) * v + weight * prev(v, 1)
+            j = f * layers + layer
+            y = (1.0 - weight) * v + weight * prev(v, 1)
+            turned = take(y, source)
+            rot[j] = turned
+            send_a_of(j).start()
+            packed = turned[:rows4]
+            for q in range(1, 4):
+                part = pltpu.roll(turned[q * rows4 : (q + 1) * rows4], q * quarter, 1)
+                packed = jnp.where(lane_q >= q * quarter, part, packed)
+            tail[j] = packed
+            send_b_of(j).start()
         return carry
 
     lax.fori_loop(0, layers, interior, 0)
@@ -200,8 +232,6 @@
             c.wait_recv()
         for c in to_up:
             c.wait_send()
-
-    weight, shift = weight_b[...], shift_b[...]
 
     row_s = iota((4 * EDGE, width), 0)
     keep_s = jnp.logical_and(
@@ -239,9 +269,6 @@
     use_l = jnp.logical_and(jnp.logical_not(on_right), k16 < 7)
     use_r = jnp.logical_and(on_right, k16 >= NINE)
 
-    def take(x, index):
-        return jnp.take_along_axis(x, index, axis=1, mode="promise_in_bounds")
-
     def columns(slab):
         index = NINE * slab + offset
         mine = jnp.where(on_right, take(own_hi[...], index), take(own_lo[...], index))
@@ -266,62 +293,91 @@
         v, p = v[EDGE : EDGE + rows], prev(v, 1)[EDGE : EDGE + rows]
         cols_y.append((1.0 - weight) * v + weight * p)
 
+    slab_l = (lane_r * 57) >> 9
+    m9 = lane_r - NINE * slab_l
+    field_l, layer_l = slab_l // layers, slab_l % layers
+    at = 64 * (field_l & 1) + 32 * layer_l + jnp.where(m9 < 5, m9 + 7, m9 + 16)
+    at = at & (width - 1)
+    s_tile = take(cols_y[tiles - 1], at)
+    for t in range(tiles - 2, -1, -1):
+        s_tile = jnp.where(field_l < 2 * (t + 1), take(cols_y[t], at), s_tile)
+    seam[0] = s_tile
+
+    first = sub8 < half
+
+    def outer(x):
+        return jnp.where(first, x[:EDGE], x[rows - EDGE :])
+
+    w8, source8, lane8 = outer(weight), outer(source), iota((EDGE, width), 1)
+    shift8 = outer(shift)
+    spare = [None] * slabs
     for layer in range(layers):
         js = [f * layers + layer for f in range(fields)]
         values = transport([strip(j) for j in js], lambda n, k: coef_s[layer, k])
         for j, v in zip(js, values):
             p = prev(v, 1)
-            for lo_row, at, first in ((EDGE, 0, True), (2 * EDGE, rows - EDGE, False)):
-                w = weight[at : at + EDGE]
-                y = (1.0 - w) * v[lo_row : lo_row + EDGE] + w * p[lo_row : lo_row + EDGE]
-                keep = sub8 < half if first else sub8 >= half
-                inner[j, at : at + EDGE, :] = jnp.where(keep, y, inner[j, at : at + EDGE, :])
-
-    source = (lane_r - shift) & (width - 1)
+            v8 = jnp.where(first, v[EDGE : 2 * EDGE], v[2 * EDGE : 3 * EDGE])
+            p8 = jnp.where(first, p[EDGE : 2 * EDGE], p[2 * EDGE : 3 * EDGE])
+            spare[j] = take((1.0 - w8) * v8 + w8 * p8, source8)
+            brim[j] = spare[j]
+    groups = (slabs + 3) // 4
+    for u in range(groups):
+        packed = spare[4 * u]
+        for q in range(1, min(4, slabs - 4 * u)):
+            packed = jnp.where(
+                lane8 >= q * quarter, pltpu.roll(spare[4 * u + q], q * quarter, 1), packed
+            )
+        brim_tail[u] = packed
+
+    late = [
+        remote(seam.at[0], seam.at[1], 12, right, rad),
+        remote(brim, got_brim, 13, right, rad),
+        remote(seam.at[0], seam.at[2], 14, right2, rad),
+        remote(brim_tail, got_brim_tail, 15, right2, rad),
+    ]
+    for c in late:
+        c.start()
+
     in_strip = jnp.logical_or(source <= 4, source >= width - 4)
-    strip_lane = jnp.where(source < width // 2, source + 7, source - (width - NINE) + 16)
-
-    def send_a_of(j):
-        return pltpu.make_async_remote_copy(
-            src_ref=rot.at[j], dst_ref=got.at[j], send_sem=send_a.at[j], recv_sem=recv_a.at[j],
-            device_id=dev(right, rad), device_id_type=pl.DeviceIdType.MESH,
-        )
-
-    def send_b_of(j):
-        return pltpu.make_async_remote_copy(
-            src_ref=tail.at[j], dst_ref=got_tail.at[j], send_sem=send_b.at[j], recv_sem=recv_b.at[j],
-            device_id=dev(right2, rad), device_id_type=pl.DeviceIdType.MESH,
-        )
-
-    quarter = width // 4
-    rows4 = rows // 4
-
-    lane_q = lane_r[:rows4]
-    for f in range(fields):
-        for layer in range(layers):
-            j = f * layers + layer
-            at = (strip_lane + (64 * (f % 2) + 32 * layer)) & (width - 1)
-            turned = jnp.where(in_strip, take(cols_y[f // 2], at), take(inner[j], source))
-            rot[j] = turned
-            send_a_of(j).start()
-            packed = turned[:rows4]
-            for q in range(1, 4):
-                part = pltpu.roll(turned[q * rows4 : (q + 1) * rows4], q * quarter, 1)
-                packed = jnp.where(lane_q >= q * quarter, part, packed)
-            tail[j] = packed
-            send_b_of(j).start()
-
-    def finish(j, carry):
+    seam_lane = jnp.where(source <= 4, source, source - (width - NINE))
+    here, next_ = lane_r >= shift, lane_r >= shift - width
+    here8, next8 = lane8 >= shift8, lane8 >= shift8 - width
+
+    def gather(j, carry):
         send_a_of(j).wait_recv()
         send_b_of(j).wait_recv()
         b = got_tail[j]
         parts = [b] + [pltpu.roll(b, width - q * quarter, 1) for q in range(1, 4)]
         far = jnp.concatenate(parts, axis=0)
-        near = jnp.where(lane_r >= shift - width, got[j], far)
-        out[j] = jnp.where(lane_r >= shift, rot[j], near)
+        out[j] = jnp.where(here, rot[j], jnp.where(next_, got[j], far))
         return carry
 
-    lax.fori_loop(0, slabs, finish, 0)
+    lax.fori_loop(0, slabs, gather, 0)
+    for c in late:
+        c.wait_recv()
+
+    for j in range(slabs):
+        at = (NINE * j + seam_lane) & (width - 1)
+        patch = jnp.where(
+            here, take(seam[0], at), jnp.where(next_, take(seam[1], at), take(seam[2], at))
+        )
+        q = j % 4
+        far8 = got_brim_tail[j // 4]
+        if q:
+            far8 = pltpu.roll(far8, width - q * quarter, 1)
+        rim = jnp.where(here8, brim[j], jnp.where(next8, got_brim[j], far8))
+        base = jnp.concatenate(
+            [
+                jnp.where(first, rim, out[j, :EDGE]),
+                out[j, EDGE : rows - EDGE],
+                jnp.where(first, out[j, rows - EDGE :], rim),
+            ],
+            axis=0,
+        )
+        out[j] = jnp.where(in_strip, patch, base)
+
+    for c in late:
+        c.wait_send()
 
     def drain(j, carry):
         send_a_of(j).wait_send()
@@ -343,7 +399,7 @@
     vmem = pl.BlockSpec(memory_space=pltpu.VMEM)
     result = pl.pallas_call(
         functools.partial(kernel, n_az, n_rad, fields, layers),
-        out_shape=jax.ShapeDtypeStruct((slabs, rows, width), f32),
+        out_shape=pltpu.VMEM((slabs, rows, width), f32),
         in_specs=[hbm, hbm, hbm, hbm],
         out_specs=vmem,
         scratch_shapes=[
@@ -363,12 +419,16 @@
             pltpu.VMEM((layers, 5, rows, width), f32),
             pltpu.VMEM((layers, 5, 4 * EDGE, width), f32),
             pltpu.VMEM((5, tall, width), f32),
-            pltpu.VMEM((slabs, rows, width), f32),
+            pltpu.VMEM((3, rows, width), f32),
+            pltpu.VMEM((slabs, EDGE, width), f32),
+            pltpu.VMEM((slabs, EDGE, width), f32),
+            pltpu.VMEM(((slabs + 3) // 4, EDGE, width), f32),
+            pltpu.VMEM(((slabs + 3) // 4, EDGE, width), f32),
             pltpu.VMEM((slabs, rows, width), f32),
             pltpu.VMEM((slabs, rows // 4, width), f32),
             pltpu.VMEM((slabs, rows, width), f32),
             pltpu.VMEM((slabs, rows // 4, width), f32),
-            dma((4,)), dma((12,)), dma((12,)),
+            dma((4,)), dma((16,)), dma((16,)),
             dma((slabs,)), dma((slabs,)), dma((slabs,)), dma((slabs,)),
         ],
         compiler_params=pltpu.CompilerParams(

time: 22.7 us -> 20.1 us (0.89)
  the two profiles are of different devices: /device:TPU:0 before, /device:TPU:2 now
where the time goes in v3:
time: 20.1 us; the launch traced here: 19.9 us
  Pallas kernels  19.2 us (96%)
  local copies, waits for them, and re-layouts  0.73 us (4%)
    pallas_call x1, Pallas kernels, on_device(): pl.pallas_call(functools.partial(kernel, n_az, n_rad, fields, layers), ou...  19.2 us
    unnamed x1, local copies, waits for them, and re-layouts  0.73 us

profile of v3, /device:TPU:2, one launch (start us, length us, event | category | flops | bytes accessed | tf_op | source)
XLA Modules:
  0.0 19.9 jit_solution(6185434359271062040)
XLA Ops:
  0.0 19.2 %shard_map.46 = f32[10,64,128]{2,1,0:T(8,128)S(1)} custom-call(f32[10,64,128]{2,1,0:T(8,128)} %bitcast.6, f32[4,64,128]{2,1,0:T(8,128)} %bitcast.7, s32[1,64]{1,0:T(1,128)} %bitcast.8, f32[1,64]{1,0:T(1,128)} %bitcast.9), custom_call_target="tpu_custom_call" | custom-call | flops 50000000 | bytes 800000 | tf_op jit(solution)/shard_map/pallas_call | solution.py:400
  19.2 0.7 %copy.6 = f32[5,2,64,128]{3,2,1,0:T(8,128)} copy(f32[5,2,64,128]{3,2,1,0:T(8,128)S(1)} %bitcast.5) | data formatting | bytes 655360

commit v4 on v3

--- a/solution.py
+++ b/solution.py
@@ -16,8 +16,8 @@
     n_az, n_rad, fields, layers,
     fluid, vel, shift_hbm, frac_hbm, out,
     shift_ref, frac_ref, shift_b, weight_b, xin, own_lo, own_hi, row_lo, row_hi, halo_l, halo_r, halo_d, halo_u,
-    coef, coef_s, coef_t, seam, brim, got_brim, brim_tail, got_brim_tail, rot, tail, got, got_tail,
-    in_sem, send_h, recv_h, send_a, recv_a, send_b, recv_b,
+    coef, coef_s, coef_t, seam, brim, got_brim, brim_tail, got_brim_tail, rot, tail, got, got_tail, relayed,
+    in_sem, send_h, recv_h, send_a, recv_a, send_b, recv_b, send_f, recv_f,
 ):
     slabs = fields * layers
     vels = 2 * layers
@@ -190,6 +190,15 @@
         )
 
 
+    even = lax.rem(az, 2) == 0
+    is_even = jnp.full((rows, width), lax.rem(az, 2), jnp.int32) == 0
+
+    def relay_of(j):
+        return pltpu.make_async_remote_copy(
+            src_ref=got.at[j], dst_ref=relayed.at[j], send_sem=send_f.at[j], recv_sem=recv_f.at[j],
+            device_id=dev(right, rad), device_id_type=pl.DeviceIdType.MESH,
+        )
+
     def take(x, index):
         return jnp.take_along_axis(x, index, axis=1, mode="promise_in_bounds")
 
@@ -211,7 +220,6 @@
                 part = pltpu.roll(turned[q * rows4 : (q + 1) * rows4], q * quarter, 1)
                 packed = jnp.where(lane_q >= q * quarter, part, packed)
             tail[j] = packed
-            send_b_of(j).start()
         return carry
 
     lax.fori_loop(0, layers, interior, 0)
@@ -338,17 +346,39 @@
     for c in late:
         c.start()
 
+    @pl.when(even)
+    def _():
+        for j in range(slabs):
+            send_b_of(j).start()
+
     in_strip = jnp.logical_or(source <= 4, source >= width - 4)
     seam_lane = jnp.where(source <= 4, source, source - (width - NINE))
     here, next_ = lane_r >= shift, lane_r >= shift - width
     here8, next8 = lane8 >= shift8, lane8 >= shift8 - width
 
+    def relay(j, carry):
+        send_a_of(j).wait_recv()
+
+        @pl.when(even)
+        def _():
+            relay_of(j).start()
+
+        return carry
+
+    lax.fori_loop(0, slabs, relay, 0)
+
     def gather(j, carry):
-        send_a_of(j).wait_recv()
-        send_b_of(j).wait_recv()
+        @pl.when(even)
+        def _():
+            send_b_of(j).wait_recv()
+
+        @pl.when(jnp.logical_not(even))
+        def _():
+            relay_of(j).wait_recv()
+
         b = got_tail[j]
         parts = [b] + [pltpu.roll(b, width - q * quarter, 1) for q in range(1, 4)]
-        far = jnp.concatenate(parts, axis=0)
+        far = jnp.where(is_even, jnp.concatenate(parts, axis=0), relayed[j])
         out[j] = jnp.where(here, rot[j], jnp.where(next_, got[j], far))
         return carry
 
@@ -381,7 +411,12 @@
 
     def drain(j, carry):
         send_a_of(j).wait_send()
-        send_b_of(j).wait_send()
+
+        @pl.when(even)
+        def _():
+            send_b_of(j).wait_send()
+            relay_of(j).wait_send()
+
         return carry
 
     lax.fori_loop(0, slabs, drain, 0)
@@ -428,8 +463,9 @@
             pltpu.VMEM((slabs, rows // 4, width), f32),
             pltpu.VMEM((slabs, rows, width), f32),
             pltpu.VMEM((slabs, rows // 4, width), f32),
+            pltpu.VMEM((slabs, rows, width), f32),
             dma((4,)), dma((16,)), dma((16,)),
-            dma((slabs,)), dma((slabs,)), dma((slabs,)), dma((slabs,)),
+            dma((slabs,)), dma((slabs,)), dma((slabs,)), dma((slabs,)), dma((slabs,)), dma((slabs,)),
         ],
         compiler_params=pltpu.CompilerParams(
             collective_id=0, has_side_effects=True, vmem_limit_bytes=60 * 1024 * 1024

time: 20.1 us -> 19.2 us (0.955)
  Pallas kernels: 19.2 us -> 18.3 us
    pallas_call x1, Pallas kernels: 19.2 us -> 18.3 us  [on_device(): pl.pallas_call(functools.partial(kernel, n_az, n_rad, fields, layers), ou...]
where the time goes in v4:
time: 19.2 us; the launch traced here: 19 us
  Pallas kernels  18.3 us (95%)
  local copies, waits for them, and re-layouts  0.73 us (4%)
    pallas_call x1, Pallas kernels, on_device(): pl.pallas_call(functools.partial(kernel, n_az, n_rad, fields, layers), ou...  18.3 us
    unnamed x1, local copies, waits for them, and re-layouts  0.73 us

profile of v4, /device:TPU:2, one launch (start us, length us, event | category | flops | bytes accessed | tf_op | source)
XLA Modules:
  0.0 19.0 jit_solution(7825864212558447278)
XLA Ops:
  0.0 18.3 %shard_map.46 = f32[10,64,128]{2,1,0:T(8,128)S(1)} custom-call(f32[10,64,128]{2,1,0:T(8,128)} %bitcast.6, f32[4,64,128]{2,1,0:T(8,128)} %bitcast.7, s32[1,64]{1,0:T(1,128)} %bitcast.8, f32[1,64]{1,0:T(1,128)} %bitcast.9), custom_call_target="tpu_custom_call" | custom-call | flops 50000000 | bytes 800000 | tf_op jit(solution)/shard_map/pallas_call | solution.py:435
  18.3 0.7 %copy.6 = f32[5,2,64,128]{3,2,1,0:T(8,128)} copy(f32[5,2,64,128]{3,2,1,0:T(8,128)S(1)} %bitcast.5) | data formatting | bytes 655360

commit v5 on v4

--- a/solution.py
+++ b/solution.py
@@ -224,22 +224,18 @@
 
     lax.fori_loop(0, layers, interior, 0)
 
-    for c in sides:
-        c.wait()
+    corner_up, corner_dn = to_up.pop(1), to_dn.pop(1)
+    sides[0].wait_recv()
 
     @pl.when(has_dn)
     def _():
         for c in to_up:
             c.wait_recv()
-        for c in to_dn:
-            c.wait_send()
 
     @pl.when(has_up)
     def _():
         for c in to_dn:
             c.wait_recv()
-        for c in to_up:
-            c.wait_send()
 
     row_s = iota((4 * EDGE, width), 0)
     keep_s = jnp.logical_and(
@@ -263,53 +259,48 @@
     keep_t = jnp.logical_and(
         jnp.logical_or(row_t >= EDGE, has_dn), jnp.logical_or(row_t < EDGE + rows, has_up)
     )
-    k16 = lane_t & 15
-    group = lane_t >> 4
-    on_right = (group & 1) == 1
-    layer_of = (group >> 1) & 1
-    part_of = group >> 2
-    lag = NINE - 7
-    offset = jnp.where(
-        on_right,
-        jnp.where(k16 < NINE, k16, k16 - NINE),
-        jnp.where(k16 < 7, k16 + lag, k16 - 7),
-    )
-    use_l = jnp.logical_and(jnp.logical_not(on_right), k16 < 7)
-    use_r = jnp.logical_and(on_right, k16 >= NINE)
-
-    def columns(slab):
-        index = NINE * slab + offset
-        mine = jnp.where(on_right, take(own_hi[...], index), take(own_lo[...], index))
-        x = jnp.where(use_l, take(halo_l[...], index), mine)
-        x = jnp.where(use_r, take(halo_r[...], index), x)
-        return jnp.where(keep_t, x, 0.0)
-
-    cs = coefficients(
-        columns(slabs + layer_of), columns(slabs + layers + layer_of), keep_t
-    )
-    for k in range(5):
-        coef_t[k] = cs[k]
-
+    k32 = lane_t & 31
+    group = lane_t >> 5
+    layer_of = group & 1
+    part_of = group >> 1
+    lower = k32 < NINE
+    offset = jnp.where(lower, k32, k32 - NINE)
     tiles = (fields + 1) // 2
-    cols = [
-        columns(jnp.minimum(2 * t + part_of, fields - 1) * layers + layer_of)
-        for t in range(tiles)
-    ]
-    cols = transport(cols, lambda n, k: coef_t[k])
-    cols_y = []
-    for v in cols:
-        v, p = v[EDGE : EDGE + rows], prev(v, 1)[EDGE : EDGE + rows]
-        cols_y.append((1.0 - weight) * v + weight * p)
+
+    def seam_columns(before_ref, after_ref, side):
+        def columns(slab):
+            index = (NINE * slab + offset) & (width - 1)
+            x = jnp.where(lower, take(before_ref[...], index), take(after_ref[...], index))
+            return jnp.where(keep_t, x, 0.0)
+
+        cs = coefficients(
+            columns(slabs + layer_of), columns(slabs + layers + layer_of), keep_t
+        )
+        for k in range(5):
+            coef_t[side, k] = cs[k]
+        cols = [
+            columns(jnp.minimum(2 * t + part_of, fields - 1) * layers + layer_of)
+            for t in range(tiles)
+        ]
+        cols = transport(cols, lambda n, k: coef_t[side, k])
+        cols_y = []
+        for v in cols:
+            v, p = v[EDGE : EDGE + rows], prev(v, 1)[EDGE : EDGE + rows]
+            cols_y.append((1.0 - weight) * v + weight * p)
+        return cols_y
 
     slab_l = (lane_r * 57) >> 9
     m9 = lane_r - NINE * slab_l
     field_l, layer_l = slab_l // layers, slab_l % layers
-    at = 64 * (field_l & 1) + 32 * layer_l + jnp.where(m9 < 5, m9 + 7, m9 + 16)
-    at = at & (width - 1)
-    s_tile = take(cols_y[tiles - 1], at)
-    for t in range(tiles - 2, -1, -1):
-        s_tile = jnp.where(field_l < 2 * (t + 1), take(cols_y[t], at), s_tile)
-    seam[0] = s_tile
+
+    def seam_tile(cols_y, first_k):
+        at = (64 * (field_l & 1) + 32 * layer_l + m9 + first_k) & (width - 1)
+        x = take(cols_y[tiles - 1], at)
+        for t in range(tiles - 2, -1, -1):
+            x = jnp.where(field_l < 2 * (t + 1), take(cols_y[t], at), x)
+        return x
+
+    seam[0] = seam_tile(seam_columns(halo_l, own_lo, 0), 5)
 
     first = sub8 < half
 
@@ -340,7 +331,6 @@
     late = [
         remote(seam.at[0], seam.at[1], 12, right, rad),
         remote(brim, got_brim, 13, right, rad),
-        remote(seam.at[0], seam.at[2], 14, right2, rad),
         remote(brim_tail, got_brim_tail, 15, right2, rad),
     ]
     for c in late:
@@ -351,9 +341,35 @@
         for j in range(slabs):
             send_b_of(j).start()
 
+    sides[1].wait_recv()
+
+    @pl.when(has_dn)
+    def _():
+        corner_up.wait_recv()
+        for c in to_dn + [corner_dn]:
+            c.wait_send()
+
+    @pl.when(has_up)
+    def _():
+        corner_dn.wait_recv()
+        for c in to_up + [corner_up]:
+            c.wait_send()
+
+    for c in sides:
+        c.wait_send()
+    seam[2] = seam_tile(seam_columns(own_hi, halo_r, 1), 0)
+
     in_strip = jnp.logical_or(source <= 4, source >= width - 4)
-    seam_lane = jnp.where(source <= 4, source, source - (width - NINE))
     here, next_ = lane_r >= shift, lane_r >= shift - width
+    low = source <= 4
+    seam_lane = jnp.where(
+        low, source + 4, jnp.where(here, source - (width - NINE), source - (width - 4))
+    )
+    at_end = jnp.logical_and(here, jnp.logical_not(low))
+    mine = jnp.logical_or(
+        jnp.logical_and(here, low),
+        jnp.logical_and(jnp.logical_not(jnp.logical_or(here, low)), next_),
+    )
     here8, next8 = lane8 >= shift8, lane8 >= shift8 - width
 
     def relay(j, carry):
@@ -389,7 +405,7 @@
     for j in range(slabs):
         at = (NINE * j + seam_lane) & (width - 1)
         patch = jnp.where(
-            here, take(seam[0], at), jnp.where(next_, take(seam[1], at), take(seam[2], at))
+            mine, take(seam[0], at), jnp.where(at_end, take(seam[2], at), take(seam[1], at))
         )
         q = j % 4
         far8 = got_brim_tail[j // 4]
@@ -453,7 +469,7 @@
             pltpu.VMEM((total // 2, EDGE, width), f32),
             pltpu.VMEM((layers, 5, rows, width), f32),
             pltpu.VMEM((layers, 5, 4 * EDGE, width), f32),
-            pltpu.VMEM((5, tall, width), f32),
+            pltpu.VMEM((2, 5, tall, width), f32),
             pltpu.VMEM((3, rows, width), f32),
             pltpu.VMEM((slabs, EDGE, width), f32),
             pltpu.VMEM((slabs, EDGE, width), f32),

time: 19.2 us -> 17.5 us (0.911)
  the two profiles are of different devices: /device:TPU:2 before, /device:TPU:0 now
where the time goes in v5:
time: 17.5 us; the launch traced here: 17.4 us
  Pallas kernels  16.7 us (95%)
  local copies, waits for them, and re-layouts  0.73 us (4%)
    pallas_call x1, Pallas kernels, on_device(): pl.pallas_call(functools.partial(kernel, n_az, n_rad, fields, layers), ou...  16.7 us
    unnamed x1, local copies, waits for them, and re-layouts  0.73 us

profile of v5, /device:TPU:0, one launch (start us, length us, event | category | flops | bytes accessed | tf_op | source)
XLA Modules:
  0.0 17.4 jit_solution(3447183809352891954)
XLA Ops:
  0.0 16.7 %shard_map.46 = f32[10,64,128]{2,1,0:T(8,128)S(1)} custom-call(f32[10,64,128]{2,1,0:T(8,128)} %bitcast.6, f32[4,64,128]{2,1,0:T(8,128)} %bitcast.7, s32[1,64]{1,0:T(1,128)} %bitcast.8, f32[1,64]{1,0:T(1,128)} %bitcast.9), custom_call_target="tpu_custom_call" | custom-call | flops 50000000 | bytes 800000 | tf_op jit(solution)/shard_map/pallas_call | solution.py:451
  16.7 0.7 %copy.6 = f32[5,2,64,128]{3,2,1,0:T(8,128)} copy(f32[5,2,64,128]{3,2,1,0:T(8,128)S(1)} %bitcast.5) | data formatting | bytes 655360

commit v6 on v5

--- a/solution.py
+++ b/solution.py
@@ -36,6 +36,20 @@
     def dev(a, r):
         return {"az": a, "rad": r}
 
+    barrier = pltpu.get_barrier_semaphore()
+    for a in (right, left, left2):
+        pl.semaphore_signal(barrier, inc=1, device_id=dev(a, rad))
+
+    @pl.when(has_dn)
+    def _():
+        for a in (right, left, az):
+            pl.semaphore_signal(barrier, inc=1, device_id=dev(a, rad - 1))
+
+    @pl.when(has_up)
+    def _():
+        for a in (right, left, az):
+            pl.semaphore_signal(barrier, inc=1, device_id=dev(a, rad + 1))
+
     load_f = pltpu.make_async_copy(fluid, xin.at[pl.ds(0, slabs)], in_sem.at[0])
     load_v = pltpu.make_async_copy(vel, xin.at[pl.ds(slabs, vels)], in_sem.at[1])
     load_s = pltpu.make_async_copy(shift_hbm, shift_ref, in_sem.at[2])
@@ -43,20 +57,6 @@
     loads = (load_s, load_w, load_f, load_v)
     for c in loads:
         c.start()
-
-    barrier = pltpu.get_barrier_semaphore()
-    for a in (left, right, left2):
-        pl.semaphore_signal(barrier, inc=1, device_id=dev(a, rad))
-
-    @pl.when(has_dn)
-    def _():
-        for a in (left, az, right):
-            pl.semaphore_signal(barrier, inc=1, device_id=dev(a, rad - 1))
-
-    @pl.when(has_up)
-    def _():
-        for a in (left, az, right):
-            pl.semaphore_signal(barrier, inc=1, device_id=dev(a, rad + 1))
 
     quarter = width // 4
     rows4 = rows // 4
@@ -301,6 +301,8 @@
         return x
 
     seam[0] = seam_tile(seam_columns(halo_l, own_lo, 0), 5)
+    late_seam = remote(seam.at[0], seam.at[1], 12, right, rad)
+    late_seam.start()
 
     first = sub8 < half
 
@@ -329,12 +331,12 @@
         brim_tail[u] = packed
 
     late = [
-        remote(seam.at[0], seam.at[1], 12, right, rad),
         remote(brim, got_brim, 13, right, rad),
         remote(brim_tail, got_brim_tail, 15, right2, rad),
     ]
     for c in late:
         c.start()
+    late.append(late_seam)
 
     @pl.when(even)
     def _():

time: 17.5 us -> 17.6 us (level)
  no operation moved by 1% of the time
where the time goes in v6:
time: 17.6 us; the launch traced here: 17.5 us
  Pallas kernels  16.7 us (95%)
  local copies, waits for them, and re-layouts  0.73 us (4%)
    pallas_call x1, Pallas kernels, on_device(): pl.pallas_call(functools.partial(kernel, n_az, n_rad, fields, layers), ou...  16.7 us
    unnamed x1, local copies, waits for them, and re-layouts  0.73 us

profile of v6, /device:TPU:0, one launch (start us, length us, event | category | flops | bytes accessed | tf_op | source)
XLA Modules:
  0.0 17.5 jit_solution(9588248654800251672)
XLA Ops:
  0.0 16.7 %shard_map.46 = f32[10,64,128]{2,1,0:T(8,128)S(1)} custom-call(f32[10,64,128]{2,1,0:T(8,128)} %bitcast.6, f32[4,64,128]{2,1,0:T(8,128)} %bitcast.7, s32[1,64]{1,0:T(1,128)} %bitcast.8, f32[1,64]{1,0:T(1,128)} %bitcast.9), custom_call_target="tpu_custom_call" | custom-call | flops 50000000 | bytes 800000 | tf_op jit(solution)/shard_map/pallas_call | solution.py:453
  16.7 0.7 %copy.6 = f32[5,2,64,128]{3,2,1,0:T(8,128)} copy(f32[5,2,64,128]{3,2,1,0:T(8,128)S(1)} %bitcast.5) | data formatting | bytes 655360
